TPU v7x, 32 devices: a whole 2x2x4 slice. The times are simulated.
32 devices in a mesh: video: 4 (over y, x), tm: 8 (over z, core).
Axes of the slice: x: 2, y: 2, z: 4, core: 2. Of those that a mesh axis runs over, the one named last changes fastest.
Arguments:
- bin_grad: bfloat16 [16, 32, 16, 1024], P('video', 'tm'), may hold values from -0.125 to 0.125
- tap_weight: float32 [16, 32, 16, 2], P('video', 'tm'), may hold values from 0.05 to 1
- tap_index: int32 [16, 32, 16, 2], P('video', 'tm'), may hold values from 0 to 1023, as said below
- features: bfloat16 [16, 1024, 1024], P('video', 'tm'), may hold values from -6 to 6
- preact: bfloat16 [16, 1024, 1024], P('video', 'tm'), may hold values from -8 to 8
- filter_second: bfloat16 [3, 1024, 1024], replicated, may hold values from -0.109375 to 0.109375
Outputs:
- first_filter_grad: float32 [1024, 3, 1024], P('tm')
- second_filter_grad: float32 [1024, 3, 1024], P('tm')
Inputs may be any that keep to these rules, and one draw needn't show every extreme that they name: `tap_index`: each proposal spans the integer snippets a to a + L for a start a and a length L of 1 or more; the taps of bin b are a + ((2 b + 1) L) // 32 and that snippet plus one. For the proposals held by one device (its 4 videos and 4 proposals of each), at most 64 taps fall into any one block of 128 snippets (snippets 128 * m to 128 * m + 127, taken over its videos together), and exactly 64 into some block.
All inputs are finite; a program needn't handle non-finite values.
Results may differ from a plain program's by a relative error of at most 0.0048.
Values may be sent and summed in bfloat16 or wider, within the bound.
A program may use at most 192 MiB of HBM per device.

v0:
```python
import jax
import jax.numpy as jnp
from jax import lax
from jax.sharding import PartitionSpec as P


def with_halo(shard, sides, width):
    for axis, dim in sides:
        count, length = (lax.axis_size(axis), shard.shape[dim])
        up = [(i, (i + 1) % count) for i in range(count - 1)]
        down = [(j, i) for i, j in up]
        last = lax.slice_in_dim(shard, length - width, length, axis=dim)
        leading = lax.slice_in_dim(shard, 0, width, axis=dim)
        before = lax.ppermute(last, axis, up)
        after = lax.ppermute(leading, axis, down)
        shard = jnp.concatenate([before, shard, after], axis=dim)
    return shard


def silu_slope(values):
    sigma = jax.nn.sigmoid(values)
    return sigma * (1.0 + values * (1.0 - sigma))


def filter_terms(layer_pairs, row_count, snip_count):
    blocks = []
    for padded, gradients in layer_pairs:
        for lag_index in range(3):
            window = padded[:, lag_index : lag_index + snip_count, :].reshape(-1, row_count)
            blocks.append(
                lax.dot_general(
                    window, gradients, (((0,), (0,)), ((), ())), preferred_element_type=jnp.float32
                )
            )
    return jnp.stack(blocks, axis=1)


def reduce_filters(layer_pairs, channels, snip_count):
    tm_total = lax.axis_size("tm")
    rows_each = channels // tm_total
    share_rows = lax.psum_scatter(
        filter_terms(layer_pairs, rows_each * lax.axis_size("tm"), snip_count),
        "tm",
        scatter_dimension=0,
        tiled=True,
    )
    return lax.psum(share_rows, "video")


def on_device(bin_grad, tap_weight, tap_index, features, preact, filter_second):
    video_count, prop_count, bin_count, tap_count = tap_index.shape
    snip_count = features.shape[1]
    channels = features.shape[2]
    peers = lax.axis_size("tm")
    unit_count = video_count * prop_count * bin_count * tap_count
    capacity = bin_count * tap_count * ((video_count * prop_count + peers - 1) // peers)
    scaled = tap_weight[..., None] * bin_grad[:, :, :, None, :].astype(jnp.float32)
    tap_rows = scaled.astype(jnp.bfloat16).reshape(unit_count, channels)
    target = (tap_index // snip_count).reshape(unit_count)
    video_of = lax.broadcasted_iota(jnp.int32, tap_index.shape, 0)
    local_row = (video_of * snip_count + tap_index % snip_count).reshape(unit_count)
    peer_hits = (target[:, None] == jnp.arange(peers, dtype=jnp.int32)[None, :]).astype(jnp.int32)
    before = jnp.cumsum(peer_hits, axis=0) - peer_hits
    position = jnp.sum(before * peer_hits, axis=1)
    slot_index = target * capacity + position
    matches = slot_index[None, :] == jnp.arange(peers * capacity, dtype=jnp.int32)[:, None]
    send_rows = jnp.dot(
        matches.astype(jnp.bfloat16), tap_rows, preferred_element_type=jnp.float32
    ).astype(jnp.bfloat16)
    send_index = jnp.max(jnp.where(matches, local_row[None, :], -1), axis=1)
    got_rows, got_index = (
        lax.all_to_all(
            send_rows.reshape(peers, capacity, channels),
            "tm",
            split_axis=0,
            concat_axis=0,
            tiled=True,
        ),
        lax.all_to_all(
            send_index.reshape(peers, capacity), "tm", split_axis=0, concat_axis=0, tiled=True
        ),
    )
    gather_table = (
        got_index.reshape(1, -1) == jnp.arange(video_count * snip_count, dtype=jnp.int32)[:, None]
    ).astype(jnp.bfloat16)
    snippet_grad = jnp.dot(
        gather_table, got_rows.reshape(-1, channels), preferred_element_type=jnp.float32
    ).astype(jnp.bfloat16)
    pre_values = preact.astype(jnp.float32)
    activation = jax.nn.silu(pre_values).astype(jnp.bfloat16)
    inputs_padded = with_halo(jnp.stack([features, activation]), (("tm", 2),), 1)
    grad_padded = with_halo(
        snippet_grad.reshape(video_count, snip_count, channels), (("tm", 1),), 1
    )
    second_pair = (inputs_padded[1], snippet_grad)
    second_filter = reduce_filters([second_pair], channels, snip_count)
    act_grad = jnp.zeros((video_count * snip_count, channels), jnp.float32)
    for lag_index in range(3):
        window = grad_padded[:, 2 - lag_index : 2 - lag_index + snip_count, :].reshape(-1, channels)
        act_grad = act_grad + lax.dot_general(
            window,
            filter_second[lag_index],
            (((1,), (1,)), ((), ())),
            preferred_element_type=jnp.float32,
        )
    pre_grad = (act_grad * silu_slope(pre_values.reshape(-1, channels))).astype(jnp.bfloat16)
    first_pair = (inputs_padded[0], pre_grad)
    first_filter = reduce_filters([first_pair], channels, snip_count)
    return (first_filter, second_filter)


def solution(mesh):
    return jax.shard_map(
        on_device,
        mesh=mesh,
        in_specs=(
            P("video", "tm", None, None),
            P("video", "tm", None, None),
            P("video", "tm", None, None),
            P("video", "tm", None),
            P("video", "tm", None),
            P(),
        ),
        out_specs=(P("tm", None, None), P("tm", None, None)),
        check_vma=False,
    )
```

profile of v0, /device:TPU:0, one launch (start us, length us, event | category | flops | bytes accessed | tf_op | source)
XLA Modules:
  0.0 430.2 jit_solution(4064759624595683488)
XLA Ops:
  7.2 0.8 fusion.24
  8.0 0.1 copy.14
  8.1 0.2 copy.13
  8.3 1.1 reduce-window.6
  9.5 0.2 slice_reduce_fusion
  9.7 0.1 reshape.84
  9.9 0.1 fusion.26
  10.0 0.2 copy.16
  10.2 0.1 broadcast_in_dim.20
  10.3 0.2 select_reduce_fusion
  10.5 0.7 all_to_all.9
  11.2 6.3 %all-to-all-start = ((s32[8,1,64]{2,1,0:T(1,128)}), s32[8,1,64]{2,1,0:T(1,128)S(1)}, u32[]{:S(2)}, u32[]{:S(2)}) async-start(s32[8,1,64]{2,1,0:T(1,128)} %all_to_all.9), calls=%async_computation | async-start | bytes 8192 | tf_op jit(solution)/shard_map/all_to_all | solution.py:79
  17.5 0.9 copy.17
  18.4 0.1 mul.54
  18.5 1.9 mul.56
  20.5 2.5 mul.57
  23.0 3.5 convolution_convert_fusion.1
  26.5 5.2 %all-to-all-start.1 = ((bf16[8,64,1024]{2,1,0:T(8,128)(2,1)}), bf16[8,64,1024]{2,1,0:T(8,128)(2,1)}, u32[]{:S(2)}, u32[]{:S(2)}) async-start(bf16[8,64,1024]{2,1,0:T(8,128)(2,1)} %bitcast.7), calls=%async_computation.1 | async-start | bytes 2097152 | tf_op jit(solution)/shard_map/all_to_all | solution.py:72
  31.7 0.6 fusion.20
  32.4 2.4 collective-permute-start
  34.8 1.3 collective-permute-start.1
  36.1 0.5 broadcast.71
  36.6 0.7 reduce.5
  37.4 1.7 collective-permute-done.1
  39.1 0.8 pad_maximum_fusion.2
  39.8 0.2 slice_bitcast_fusion
  40.0 3.1 fusion.28
  43.1 15.3 %all-to-all-done.1 = bf16[8,64,1024]{2,1,0:T(8,128)(2,1)} async-done(((bf16[8,64,1024]{2,1,0:T(8,128)(2,1)}), bf16[8,64,1024]{2,1,0:T(8,128)(2,1)}, u32[]{:S(2)}, u32[]{:S(2)}) %all-to-all-start.1) | async-done | bytes 1048608 | tf_op jit(solution)/shard_map/all_to_all | solution.py:72
  58.4 2.0 convolution_convert_fusion
  60.5 1.3 convolution_bitcast_fusion
  61.8 1.3 convolution_bitcast_fusion.2
  63.1 1.3 convolution_bitcast_fusion.1
  64.4 4.8 %pad_maximum_fusion.1 = f32[1024,3,1024]{2,0,1:T(8,128)} fusion(f32[1024,1,1024]{2,0,1:T(8,128)S(1)} %convolution_bitcast_fusion, f32[1024,1,1024]{2,0,1:T(8,128)S(1)} %convolution_bitcast_fusion.1, f32[1024,1,1024]{2,0,1:T(8,128)S(1)} %convolution_bitcast_fusion.2), kind=kLoop, calls=%fused_computation.1 | loop fusion | flops 6291456 | bytes 25165824 | tf_op jit(solution)/shard_map/stack | solution.py:35
  69.3 1.3 collective-permute-start.2
  70.6 3.2 collective-permute-start.3
  73.8 2.9 fusion.13
  76.8 0.5 pad_maximum_fusion.4
  77.2 3.4 fusion.15
  80.7 3.5 fusion.10
  84.2 1.3 convolution_bitcast_fusion.4
  85.4 1.3 convolution_bitcast_fusion.3
  86.7 1.3 convolution_bitcast_fusion.5
  88.0 4.9 %pad_maximum_fusion = f32[1024,3,1024]{2,0,1:T(8,128)} fusion(f32[1024,1,1024]{2,0,1:T(8,128)S(1)} %convolution_bitcast_fusion.3, f32[1024,1,1024]{2,0,1:T(8,128)S(1)} %convolution_bitcast_fusion.4, f32[1024,1,1024]{2,0,1:T(8,128)S(1)} %convolution_bitcast_fusion.5), kind=kLoop, calls=%fused_computation | loop fusion | flops 6291456 | bytes 25165824 | tf_op jit(solution)/shard_map/stack | solution.py:35
  93.0 107.9 %reduce-scatter.5.cloned.1.call-done = f32[128,3,1024]{2,0,1:T(8,128)} async-done(((f32[1024,3,1024]{2,0,1:T(8,128)}), f32[128,3,1024]{2,0,1:T(8,128)}) %reduce-scatter.5.cloned.1.call-update) | async-done | bytes 1572880 | tf_op jit(solution)/shard_map/reduce_scatter | solution.py:41
  200.9 129.9 %reduce-scatter.3.cloned.1.call-done = f32[128,3,1024]{2,0,1:T(8,128)} async-done(((f32[1024,3,1024]{2,0,1:T(8,128)}), f32[128,3,1024]{2,0,1:T(8,128)}) %reduce-scatter.3.cloned.1.call-update) | async-done | bytes 1572880 | tf_op jit(solution)/shard_map/reduce_scatter | solution.py:41
  330.8 88.9 %all-reduce.3.cloned.1.call-done = (f32[128,3,1024]{2,0,1:T(8,128)}, f32[128,3,1024]{2,0,1:T(8,128)}) async-done(((f32[128,3,1024]{2,0,1:T(8,128)}, f32[128,3,1024]{2,0,1:T(8,128)}), (f32[128,3,1024]{2,0,1:T(8,128)}, f32[128,3,1024]{2,0,1:T(8,128)})) %all-reduce.3.cloned.1.call-update) | async-done | bytes 3145744 | tf_op jit(solution)/shard_map/psum | solution.py:47
  419.7 2.8 copy.20
  422.6 1.1 copy.21
  (35 shorter events, 0.5 us)
Async XLA Ops:
  11.2 15.3 %all-to-all-start = ((s32[8,1,64]{2,1,0:T(1,128)}), s32[8,1,64]{2,1,0:T(1,128)S(1)}, u32[]{:S(2)}, u32[]{:S(2)}) async-start(s32[8,1,64]{2,1,0:T(1,128)} %all_to_all.9), calls=%async_computation | async-start | bytes 8192 | tf_op jit(solution)/shard_map/all_to_all | solution.py:79
  23.0 8.8 %copy-start.6 = (bf16[4,128,1024]{2,1,0:T(8,128)(2,1)S(1)}, bf16[4,128,1024]{2,1,0:T(8,128)(2,1)}, u32[]{:S(2)}) copy-start(bf16[4,128,1024]{2,1,0:T(8,128)(2,1)} %param.10) | copy-start | bytes 3145732
  26.5 5.9 %copy-start = (bf16[4,128,1024]{2,1,0:T(8,128)(2,1)S(1)}, bf16[4,128,1024]{2,1,0:T(8,128)(2,1)}, u32[]{:S(2)}) copy-start(bf16[4,128,1024]{2,1,0:T(8,128)(2,1)} %param.9) | copy-start | bytes 3145732
  26.5 31.9 %all-to-all-start.1 = ((bf16[8,64,1024]{2,1,0:T(8,128)(2,1)}), bf16[8,64,1024]{2,1,0:T(8,128)(2,1)}, u32[]{:S(2)}, u32[]{:S(2)}) async-start(bf16[8,64,1024]{2,1,0:T(8,128)(2,1)} %bitcast.7), calls=%async_computation.1 | async-start | bytes 2097152 | tf_op jit(solution)/shard_map/all_to_all | solution.py:72
  31.7 169.2 %reduce-scatter.5.cloned.1.call-start = ((), (), s32[]{:S(2)}) async-start(), calls=%async_computation.5 | async-start | bytes 14155776 | tf_op jit(solution)/shard_map/reduce_scatter | solution.py:41
  32.4 4.9 %collective-permute-start = (bf16[2,4,1,1024]{3,2,1,0:T(2,128)(2,1)S(1)}, bf16[2,4,1,1024]{3,2,1,0:T(2,128)(2,1)S(1)}, u32[]{:S(2)}, u32[]{:S(2)}) collective-permute-start(bf16[2,4,1,1024]{3,2,1,0:T(2,128)(2,1)S(1)} %get-tuple-element.6), channel_id=1, source_target_pairs={{0,1},{1,2},{2,3},{3,4},{4,5},{5,6},{6,7},{8,9},{9,10},{10,11},{11... | collective-permute-start | bytes 49160 | tf_op jit(solution)/shard_map/ppermute | solution.py:14
  34.8 4.2 collective-permute-start.1
  58.4 2.0 copy-start.5
  60.4 1.3 copy-start.4
  61.8 1.3 copy-start.3
  69.2 261.6 %reduce-scatter.3.cloned.1.call-start = ((), (), s32[]{:S(2)}) async-start(), calls=%async_computation.4 | async-start | bytes 14155776 | tf_op jit(solution)/shard_map/reduce_scatter | solution.py:41
  69.3 7.4 %collective-permute-start.2 = (bf16[4,1,1024]{2,1,0:T(2,128)(2,1)S(1)}, bf16[4,1,1024]{2,1,0:T(2,128)(2,1)S(1)}, u32[]{:S(2)}, u32[]{:S(2)}) collective-permute-start(bf16[4,1,1024]{2,1,0:T(2,128)(2,1)S(1)} %get-tuple-element.16), channel_id=1, source_target_pairs={{1,0},{2,1},{3,2},{4,3},{5,4},{6,5},{7,6},{9,8},{10,9},{11,10},{12... | collective-permute-start | bytes 24584 | tf_op jit(solution)/shard_map/ppermute | solution.py:15
  70.6 6.1 %collective-permute-start.3 = (bf16[4,1,1024]{2,1,0:T(2,128)(2,1)S(1)}, bf16[4,1,1024]{2,1,0:T(2,128)(2,1)S(1)}, u32[]{:S(2)}, u32[]{:S(2)}) collective-permute-start(bf16[4,1,1024]{2,1,0:T(2,128)(2,1)S(1)} %get-tuple-element.17), channel_id=1, source_target_pairs={{0,1},{1,2},{2,3},{3,4},{4,5},{5,6},{6,7},{8,9},{9,10},{10,11},{11... | collective-permute-start | bytes 24584 | tf_op jit(solution)/shard_map/ppermute | solution.py:14
  77.2 3.4 copy-start.7
  80.6 3.5 copy-start.2
  93.0 326.7 %all-reduce.3.cloned.1.call-start = ((), (), s32[]{:S(2)}) async-start(), calls=%async_computation.6 | async-start | bytes 6291456 | tf_op jit(solution)/shard_map/psum | solution.py:47
  419.7 2.9 copy-start.1
Sparse Core Ops, SparseCore 0:
  69.4 131.5 reduce-scatter.4
  203.2 127.5 reduce-scatter.2
  333.9 85.7 all-reduce.2
where the time goes:
time: 431 us; the launch traced here: 430 us
  waiting for transfers between devices  344 us (80%)
  matrix products  23 us (5%)
  starting transfers between devices  19.8 us (5%)
  local copies, waits for them, and re-layouts  15.1 us (4%)
  other arithmetic  14.6 us (3%)
  between operations  14 us (3%)
    reduce_scatter x2, waiting for transfers between devices, reduce_filters(): lax.psum_scatter(filter_terms(layer_pairs, rows_each * lax.axis_size('tm'...  238 us
    psum x1, waiting for transfers between devices, reduce_filters(): return lax.psum(share_rows, 'video')  88.9 us
    all_to_all x1, waiting for transfers between devices, on_device(): lax.all_to_all(send_rows.reshape(peers, capacity, channels), 'tm', split_...  15.3 us
    another operation x2, other arithmetic, filter_terms(): return jnp.stack(blocks, axis=1)  9.78 us
    dot_general x3, matrix products, on_device(): lax.dot_general(window, filter_second[lag_index], (((1,), (1,)), ((), ())...  9.76 us
  transfers between devices with their start and end apart: 9, of which 5 were waited for; matrix products, arithmetic and copies ran while one was open for 8% of the time, Pallas kernels for 0%

commit v1 on v0

v1 whole, which is shorter than its diff:
```python
import functools

import jax
import jax.numpy as jnp
from jax import lax
from jax.experimental import pallas as pl
from jax.experimental.pallas import tpu as pltpu
from jax.sharding import PartitionSpec as P

MESH = pl.DeviceIdType.MESH
UNITS = 2


def silu_slope(values):
    sigma = jax.nn.sigmoid(values)
    return sigma * (1.0 + values * (1.0 - sigma))


def reduce_kernel(tm, steps, rows, cols, q_ref, out_ref, r1, s1, r2, t2, r3, g4, r4,
                  p1_s, p1_r, p2_s, p2_r, p3_s, p3_r, p4_s, p4_r):
    depth = tm // 2
    video = lax.axis_index("video")
    here = lax.axis_index("tm")
    x, y = lax.rem(video, 2), video // 2
    core, z = lax.rem(here, 2), here // 2
    flip_x = y * 2 + (1 - x)
    flip_y = (1 - y) * 2 + x
    flip_xy = (1 - y) * 2 + (1 - x)
    others = (flip_x, flip_y, flip_xy)
    other_bits = ((1 - x, y), (x, 1 - y), (1 - x, 1 - y))
    half, quarter = cols // 4, cols // 8

    def z_peer(j):
        return lax.rem(z + 1 + j, depth) * 2 + core

    def z_slot_row(peer_z):
        return pl.multiple_of(peer_z * rows, rows)

    barrier = pltpu.get_barrier_semaphore()
    for v in others:
        pl.semaphore_signal(barrier, inc=1, device_id={"video": v}, device_id_type=MESH)
    for j in range(depth - 1):
        pl.semaphore_signal(barrier, inc=1, device_id={"tm": z_peer(j)}, device_id_type=MESH)
    pl.semaphore_wait(barrier, 3 + depth - 1)

    def bits(kind, xb, yb):
        return (xb, yb) if kind == 0 else (yb, xb)

    def first(step, kind):
        u = step * UNITS + kind
        h1, _ = bits(kind, 1 - x, 1 - y)
        col = pl.multiple_of(kind * (cols // 2) + h1 * half, 128)
        return pltpu.make_async_remote_copy(
            src_ref=q_ref.at[step, :, pl.ds(col, half)], dst_ref=r1.at[u],
            send_sem=p1_s.at[u], recv_sem=p1_r.at[u],
            device_id={"video": (flip_x, flip_y)[kind]}, device_id_type=MESH)

    def second(step, kind):
        u = step * UNITS + kind
        _, h2 = bits(kind, 1 - x, 1 - y)
        return pltpu.make_async_remote_copy(
            src_ref=s1.at[u, :, pl.ds(pl.multiple_of(h2 * quarter, 128), quarter)], dst_ref=r2.at[u],
            send_sem=p2_s.at[u], recv_sem=p2_r.at[u],
            device_id={"video": (flip_y, flip_x)[kind]}, device_id_type=MESH)

    def third(step, kind, j):
        u = step * UNITS + kind
        peer = lax.rem(z + 1 + j, depth)
        return pltpu.make_async_remote_copy(
            src_ref=t2.at[u, pl.ds(z_slot_row(peer), rows)], dst_ref=r3.at[u, j],
            send_sem=p3_s.at[u, j], recv_sem=p3_r.at[u, j],
            device_id={"tm": peer * 2 + core}, device_id_type=MESH)

    def fourth(step, kind, j):
        u = step * UNITS + kind
        return pltpu.make_async_remote_copy(
            src_ref=g4.at[u], dst_ref=r4.at[u, j],
            send_sem=p4_s.at[u, j], recv_sem=p4_r.at[u, j],
            device_id={"video": others[j]}, device_id_type=MESH)

    def column(kind, xb, yb):
        h1, h2 = bits(kind, xb, yb)
        return pl.ds(pl.multiple_of(kind * (cols // 2) + h1 * half + h2 * quarter, 128), quarter)

    for step in range(min(2, steps)):
        for kind in range(UNITS):
            first(step, kind).start()

    for turn in range(steps + 3):
        if turn + 2 < steps:
            for kind in range(UNITS):
                first(turn + 2, kind).start()
        if turn < steps:
            for kind in range(UNITS):
                u = turn * UNITS + kind
                first(turn, kind).wait_recv()
                h1, _ = bits(kind, x, y)
                col = pl.multiple_of(kind * (cols // 2) + h1 * half, 128)
                s1[u] = (q_ref[turn, :, pl.ds(col, half)].astype(jnp.float32)
                         + r1[u].astype(jnp.float32)).astype(jnp.bfloat16)
                second(turn, kind).start()
        step = turn - 1
        if 0 <= step < steps:
            for kind in range(UNITS):
                u = step * UNITS + kind
                second(step, kind).wait_recv()
                _, h2 = bits(kind, x, y)
                mine = s1[u, :, pl.ds(pl.multiple_of(h2 * quarter, 128), quarter)]
                t2[u] = (mine.astype(jnp.float32) + r2[u].astype(jnp.float32)).astype(jnp.bfloat16)
                for j in range(depth - 1):
                    third(step, kind, j).start()
        step = turn - 2
        if 0 <= step < steps:
            for kind in range(UNITS):
                u = step * UNITS + kind
                total = t2[u, pl.ds(z_slot_row(z), rows)].astype(jnp.float32)
                for j in range(depth - 1):
                    third(step, kind, j).wait_recv()
                    total = total + r3[u, j].astype(jnp.float32)
                g4[u] = total.astype(jnp.bfloat16)
                for j in range(3):
                    fourth(step, kind, j).start()
                out_ref[step, :, column(kind, x, y)] = g4[u].astype(jnp.float32)
        step = turn - 3
        if 0 <= step < steps:
            for kind in range(UNITS):
                u = step * UNITS + kind
                for j in range(3):
                    fourth(step, kind, j).wait_recv()
                    out_ref[step, :, column(kind, *other_bits[j])] = r4[u, j].astype(jnp.float32)

    for step in range(steps):
        for kind in range(UNITS):
            first(step, kind).wait_send()
            second(step, kind).wait_send()
            for j in range(depth - 1):
                third(step, kind, j).wait_send()
            for j in range(3):
                fourth(step, kind, j).wait_send()


def reduce_all(partials):
    steps, chip_rows, cols = partials.shape
    tm = lax.axis_size("tm")
    depth = tm // 2
    rows = chip_rows // depth
    n = steps * UNITS
    half, quarter = cols // 4, cols // 8
    bf = jnp.bfloat16
    dma = pltpu.SemaphoreType.DMA
    vmem = pl.BlockSpec(memory_space=pltpu.VMEM)
    return pl.pallas_call(
        functools.partial(reduce_kernel, tm, steps, rows, cols),
        out_shape=jax.ShapeDtypeStruct((steps, rows, cols), jnp.float32),
        in_specs=[vmem],
        out_specs=vmem,
        scratch_shapes=[
            pltpu.VMEM((n, chip_rows, half), bf),
            pltpu.VMEM((n, chip_rows, half), bf),
            pltpu.VMEM((n, chip_rows, quarter), bf),
            pltpu.VMEM((n, chip_rows, quarter), bf),
            pltpu.VMEM((n, depth - 1, rows, quarter), bf),
            pltpu.VMEM((n, rows, quarter), bf),
            pltpu.VMEM((n, 3, rows, quarter), bf),
            dma((n,)), dma((n,)), dma((n,)), dma((n,)),
            dma((n, depth - 1)), dma((n, depth - 1)), dma((n, 3)), dma((n, 3)),
        ],
        compiler_params=pltpu.CompilerParams(
            collective_id=0, has_side_effects=True, vmem_limit_bytes=48 * 1024 * 1024
        ),
        name="reduce_filters",
    )(partials)


def shifts(count, by):
    up = [(i, i + by) for i in range(count - by)]
    return up, [(j, i) for i, j in up]


def on_device(bin_grad, tap_weight, tap_index, features, preact, filter_second):
    video_count, prop_count, bin_count, tap_count = tap_index.shape
    snip_count = features.shape[1]
    channels = features.shape[2]
    peers = lax.axis_size("tm")
    depth = peers // 2
    rows = channels // peers
    core = lax.rem(lax.axis_index("tm"), 2)
    unit_count = video_count * prop_count * bin_count * tap_count
    capacity = bin_count * tap_count * ((video_count * prop_count + peers - 1) // peers)
    siblings = [(i, i + 1 - 2 * (i % 2)) for i in range(peers)]

    def chip_rows_of(mine, other):
        got = lax.ppermute(other, "tm", siblings)
        return jnp.concatenate(
            [jnp.where(core == 0, mine, got), jnp.where(core == 0, got, mine)], axis=1
        )

    def chip_lhs(values):
        split = values.reshape(video_count, snip_count, depth, 2, rows)
        pick = lambda c: lax.dynamic_index_in_dim(split, c, 3, keepdims=False).reshape(
            video_count, snip_count, depth * rows
        )
        return chip_rows_of(pick(core), pick(1 - core))

    pre_values = preact.astype(jnp.float32)
    activation = jax.nn.silu(pre_values).astype(jnp.bfloat16)
    lhs = jnp.stack([chip_lhs(features), chip_lhs(activation)])
    up, down = shifts(peers, 2)
    before = lax.ppermute(lhs[:, :, -1:], "tm", up)
    after = lax.ppermute(lhs[:, :, :1], "tm", down)
    lhs = jnp.concatenate([before, lhs, after], axis=2)

    scaled = tap_weight[..., None] * bin_grad[:, :, :, None, :].astype(jnp.float32)
    tap_rows = scaled.astype(jnp.bfloat16).reshape(unit_count, channels)
    target = (tap_index // snip_count).reshape(unit_count)
    video_of = lax.broadcasted_iota(jnp.int32, tap_index.shape, 0)
    local_row = (video_of * snip_count + tap_index % snip_count).reshape(unit_count)
    peer_hits = (target[:, None] == jnp.arange(peers, dtype=jnp.int32)[None, :]).astype(jnp.int32)
    earlier = jnp.cumsum(peer_hits, axis=0) - peer_hits
    position = jnp.sum(earlier * peer_hits, axis=1)
    slot_index = target * capacity + position
    matches = slot_index[None, :] == jnp.arange(peers * capacity, dtype=jnp.int32)[:, None]
    send_rows = jnp.dot(
        matches.astype(jnp.bfloat16), tap_rows, preferred_element_type=jnp.float32
    ).astype(jnp.bfloat16)
    send_index = jnp.max(jnp.where(matches, local_row[None, :], -1), axis=1)
    got_rows, got_index = (
        lax.all_to_all(
            send_rows.reshape(peers, capacity, channels),
            "tm",
            split_axis=0,
            concat_axis=0,
            tiled=True,
        ),
        lax.all_to_all(
            send_index.reshape(peers, capacity), "tm", split_axis=0, concat_axis=0, tiled=True
        ),
    )
    gather_table = (
        got_index.reshape(1, -1) == jnp.arange(video_count * snip_count, dtype=jnp.int32)[:, None]
    ).astype(jnp.bfloat16)
    snippet_grad = jnp.dot(
        gather_table, got_rows.reshape(-1, channels), preferred_element_type=jnp.float32
    ).astype(jnp.bfloat16).reshape(video_count, snip_count, channels)

    up, down = shifts(peers, 1)
    grad_before = lax.ppermute(snippet_grad[:, -1:], "tm", up)
    grad_after = lax.ppermute(snippet_grad[:, :1], "tm", down)
    grad_padded = jnp.concatenate([grad_before, snippet_grad, grad_after], axis=1)

    def filter_terms(padded, gradients):
        gradients = gradients.reshape(-1, channels)
        return [
            lax.dot_general(
                padded[:, k : k + 2 * snip_count].reshape(-1, depth * rows), gradients,
                (((0,), (0,)), ((), ())), preferred_element_type=jnp.float32,
            ).astype(jnp.bfloat16)
            for k in range(3)
        ]

    second_terms = filter_terms(lhs[1], chip_rows_of(snippet_grad, snippet_grad))
    act_grad = jnp.zeros((video_count * snip_count, channels), jnp.float32)
    for lag_index in range(3):
        window = grad_padded[:, 2 - lag_index : 2 - lag_index + snip_count, :].reshape(-1, channels)
        act_grad = act_grad + lax.dot_general(
            window,
            filter_second[lag_index],
            (((1,), (1,)), ((), ())),
            preferred_element_type=jnp.float32,
        )
    pre_grad = (act_grad * silu_slope(pre_values.reshape(-1, channels))).astype(jnp.bfloat16)
    pre_grad = pre_grad.reshape(video_count, snip_count, channels)
    first_terms = filter_terms(lhs[0], chip_rows_of(pre_grad, pre_grad))
    sums = reduce_all(jnp.stack(second_terms + first_terms))
    out = sums.reshape(2, 3, rows, channels).transpose(0, 2, 1, 3)
    return (out[1], out[0])


def solution(mesh):
    return jax.shard_map(
        on_device,
        mesh=mesh,
        in_specs=(
            P("video", "tm", None, None),
            P("video", "tm", None, None),
            P("video", "tm", None, None),
            P("video", "tm", None),
            P("video", "tm", None),
            P(),
        ),
        out_specs=(P("tm", None, None), P("tm", None, None)),
        check_vma=False,
    )
```

time: 431 us -> 167 us (0.39)
  waiting for transfers between devices: 344 us -> 2.31 us
  Pallas kernels: 0 us -> 79.9 us
  local copies, waits for them, and re-layouts: 15.1 us -> 32.1 us
  between operations: 14 us -> 1.04 us
  matrix products: 23 us -> 17.7 us
  other arithmetic: 14.6 us -> 10.1 us
    reduce_scatter x2 -> x0, waiting for transfers between devices: 238 us -> none  [reduce_filters(): lax.psum_scatter(filter_terms(layer_pairs, rows_each * lax.axis_size('tm'...]
    psum x1 -> x0, waiting for transfers between devices: 88.9 us -> none  [reduce_filters(): return lax.psum(share_rows, 'video')]
    pallas_call x0 -> x1, Pallas kernels: none -> 79.9 us  [reduce_all(): pl.pallas_call(functools.partial(reduce_kernel, tm, steps, rows, cols), o...]
    all_to_all x1, waiting for transfers between devices: 15.3 us -> 0.01 us  [on_device(): lax.all_to_all(send_rows.reshape(peers, capacity, channels), 'tm', split_...]
    another operation x5, other arithmetic: 11.6 us -> 2.9 us  [the longest x3 1.71 us: on_device(): lhs = jnp.stack([chip_lhs(features), chip_lhs(activation)])]
    unnamed x19 -> x21, local copies, waits for them, and re-layouts: 4.9 us -> 12.1 us
    dynamic_slice x0 -> x1, local copies, waits for them, and re-layouts: none -> 5.34 us  [chip_lhs(): lax.dynamic_index_in_dim(split, c, 3, keepdims=False)]
    dot_general x3, matrix products: 9.76 us -> 4.44 us  [on_device(): lax.dot_general(window, filter_second[lag_index], (((1,), (1,)), ((), ())...]
  transfers between devices with their start and end apart: 9 -> 10, of which waited for: 5 -> 1; matrix products, arithmetic and copies ran while one was open for 8% -> 24% of each run, Pallas kernels for 0% -> 0%
where the time goes in v1:
time: 167 us
  Pallas kernels  79.9 us (48%)
  local copies, waits for them, and re-layouts  32.1 us (19%)
  starting transfers between devices  23.6 us (14%)
  matrix products  17.7 us (11%)
  other arithmetic  10.1 us (6%)
  waiting for transfers between devices  2.31 us (1%)
    pallas_call x1, Pallas kernels, reduce_all(): pl.pallas_call(functools.partial(reduce_kernel, tm, steps, rows, cols), o...  79.9 us
    unnamed x21, local copies, waits for them, and re-layouts  12.1 us
    dot_general x6, matrix products, filter_terms(): lax.dot_general(padded[:, k:k + 2 * snip_count].reshape(-1, depth * rows)...  7.75 us
    all_to_all x1, starting transfers between devices, on_device(): lax.all_to_all(send_index.reshape(peers, capacity), 'tm', split_axis=0, c...  6.33 us
    dynamic_slice x1, local copies, waits for them, and re-layouts, chip_lhs(): lax.dynamic_index_in_dim(split, c, 3, keepdims=False)  5.34 us
    all_to_all x1, starting transfers between devices, on_device(): lax.all_to_all(send_rows.reshape(peers, capacity, channels), 'tm', split_...  5.23 us
    mul x3, local copies, waits for them, and re-layouts, on_device(): tap_weight[..., None] * bin_grad[:, :, :, None, :].astype(jnp.float32)  4.53 us
    dot_general x3, matrix products, on_device(): lax.dot_general(window, filter_second[lag_index], (((1,), (1,)), ((), ())...  4.44 us
  transfers between devices with their start and end apart: 10, of which 1 were waited for; matrix products, arithmetic and copies ran while one was open for 24% of the time, Pallas kernels for 0%

profile of v1, /device:TPU:0, one launch (start us, length us, event | category | flops | bytes accessed | tf_op | source)
XLA Modules:
  0.0 166.8 jit_solution(8835903284230128980)
XLA Ops:
  0.6 0.8 fusion.42
  1.8 1.1 reduce-window.6
  4.0 0.7 all_to_all.9
  4.7 6.3 %all-to-all-start = ((s32[8,1,64]{2,1,0:T(1,128)}), s32[8,1,64]{2,1,0:T(1,128)S(1)}, u32[]{:S(2)}, u32[]{:S(2)}) async-start(s32[8,1,64]{2,1,0:T(1,128)} %all_to_all.9), calls=%async_computation | async-start | bytes 8192 | tf_op jit(solution)/shard_map/all_to_all | solution.py:235
  11.0 0.9 copy.46
  12.0 1.9 %mul.56 = f32[4,4,16,2,1024]{4,3,2,1,0:T(2,128)S(1)} broadcast(bf16[4,4,16,1024]{3,2,1,0:T(8,128)(2,1)} %param.6), dimensions={0,1,2,4} | broadcast | bytes 2621440 | tf_op jit(solution)/shard_map/mul | solution.py:213
  13.9 2.5 %mul.57 = f32[512,1024]{1,0:T(8,128)} reshape(f32[4,4,16,2,1024]{4,3,2,1,0:T(2,128)S(1)} %mul.56) | data formatting | bytes 4194304 | tf_op jit(solution)/shard_map/mul | solution.py:213
  16.4 3.4 %convolution_convert_fusion.1 = bf16[512,1024]{1,0:T(8,128)(2,1)} fusion(f32[512,1024]{1,0:T(8,128)} %mul.57, f32[512]{0:T(512)S(1)} %mul.54, s32[512]{0:T(512)S(1)} %multiply_add_fusion), kind=kOutput, calls=%fused_computation.41 | convolution fusion | flops 538705920 | bytes 3149824 | tf_op jit(solution)/shard_map/dot_general | solution.py:223
  19.8 5.2 %all-to-all-start.1 = ((bf16[8,64,1024]{2,1,0:T(8,128)(2,1)}), bf16[8,64,1024]{2,1,0:T(8,128)(2,1)}, u32[]{:S(2)}, u32[]{:S(2)}) async-start(bf16[8,64,1024]{2,1,0:T(8,128)(2,1)} %bitcast.10), calls=%async_computation.1 | async-start | bytes 2097152 | tf_op jit(solution)/shard_map/all_to_all | solution.py:228
  25.1 0.6 fusion.3
  25.7 0.8 reshape.101
  26.5 0.8 reshape.104
  27.3 5.3 %constant_dynamic-slice_fusion.1 = (bf16[4,128,4,1,128]{4,3,2,1,0:T(2,128)(2,1)}, bf16[4,128,4,1,128]{4,3,2,1,0:T(2,128)(2,1)}, bf16[4,128,4,1,128]{4,3,2,1,0:T(2,128)(2,1)}, bf16[4,128,4,1,128]{4,3,2,1,0:T(2,128)(2,1)S(1)}) fusion(bf16[4,128,4,2,128]{4,3,2,1,0:T(2,128)(2,1)S(1)} %reshape.104, s32[]{:T(128)S(6)} %select_n.66, s32[]{:T(128)S(6)} %select_n.67, ...), kind=kLoop, calls=%fused_computation.97 | loop fusion | bytes 4194312 | tf_op jit(solution)/shard_map/jit(dynamic_index_in_dim)/dynamic_slice | solution.py:200
  32.6 3.6 %copy.48 = bf16[4,128,4,1,128]{1,4,2,0,3:T(8,128)(2,1)} copy(bf16[4,128,4,1,128]{4,3,2,1,0:T(2,128)(2,1)} %get-tuple-element.28) | data formatting | bytes 1048576
  36.2 0.5 collective-permute-start
  36.7 3.5 %copy.50 = bf16[4,128,4,1,128]{1,4,2,0,3:T(8,128)(2,1)} copy(bf16[4,128,4,1,128]{4,3,2,1,0:T(2,128)(2,1)} %get-tuple-element.25) | data formatting | bytes 1048576
  40.2 0.7 copy.49
  40.9 0.7 copy.47
  41.7 1.1 broadcast_select_fusion.7
  43.2 1.5 fusion.32
  44.6 1.6 copy.38
  46.2 3.9 %collective-permute-start.2 = (bf16[2,4,1,512]{3,1,2,0:T(4,128)(2,1)S(1)}, bf16[2,4,1,512]{3,1,2,0:T(4,128)(2,1)S(1)}, u32[]{:S(2)}, u32[]{:S(2)}) collective-permute-start(bf16[2,4,1,512]{3,1,2,0:T(4,128)(2,1)S(1)} %copy.38), channel_id=1, source_target_pairs={{0,2},{1,3},{2,4},{3,5},{4,6},{5,7},{8,10},{9,11},{10,12},{11,13},... | collective-permute-start | bytes 24584 | tf_op jit(solution)/shard_map/ppermute | solution.py:209
  50.2 0.4 copy.39
  50.5 1.5 collective-permute-start.3
  52.0 0.5 broadcast.76
  52.5 0.7 reduce.5
  53.3 0.5 copy.40
  53.8 2.3 %collective-permute-done.3 = bf16[2,4,1,512]{3,1,2,0:T(4,128)(2,1)S(1)} collective-permute-done((bf16[2,4,1,512]{3,1,2,0:T(4,128)(2,1)S(1)}, bf16[2,4,1,512]{3,1,2,0:T(4,128)(2,1)S(1)}, u32[]{:S(2)}, u32[]{:S(2)}) %collective-permute-start.3) | collective-permute-done | bytes 8224 | tf_op jit(solution)/shard_map/ppermute | solution.py:210
  56.1 1.4 copy.41
  57.5 2.1 %convolution_convert_fusion = bf16[512,1024]{1,0:T(8,128)(2,1)S(1)} fusion(bf16[512,1024]{1,0:T(8,128)(2,1)} %bitcast.11, s32[512]{0:T(512)S(1)} %eq.74), kind=kOutput, calls=%fused_computation.40 | convolution fusion | flops 537657344 | bytes 2099200 | tf_op jit(solution)/shard_map/dot_general | solution.py:242
  59.7 2.5 %pad_maximum_fusion = bf16[2,4,258,512]{2,3,1,0:T(8,128)(2,1)S(1)} fusion(bf16[2,4,1,512]{2,3,1,0:T(8,128)(2,1)S(1)} %copy-done.2, bf16[1,4,256,512]{2,3,1,0:T(8,128)(2,1)S(1)} %maximum_bitcast_fusion.1, bf16[1,4,256,512]{2,3,1,0:T(8,128)(2,1)S(1)} %maximum_bitcast_fusion, bf16[2,4,1,512]{2,3,1,0:T(8,128)(2,1)S(1)} %copy.40), kind=kLoop, calls=%fused_computation | loop fusion | flops 8454144 | bytes 4227072 | tf_op jit(solution)/shard_map/concatenate | solution.py:211
  62.1 0.3 slice_bitcast_fusion.2
  62.5 1.3 collective-permute-start.5
  63.8 3.0 %collective-permute-start.6 = (bf16[4,1,1024]{2,1,0:T(2,128)(2,1)S(1)}, bf16[4,1,1024]{2,1,0:T(2,128)(2,1)S(1)}, u32[]{:S(2)}, u32[]{:S(2)}) collective-permute-start(bf16[4,1,1024]{2,1,0:T(2,128)(2,1)S(1)} %get-tuple-element.17), channel_id=1, source_target_pairs={{0,1},{1,2},{2,3},{3,4},{4,5},{5,6},{6,7},{8,9},{9,10},{10,11},{11... | collective-permute-start | bytes 24584 | tf_op jit(solution)/shard_map/ppermute | solution.py:247
  66.9 1.3 fusion.13
  68.2 1.0 pad_maximum_fusion.4
  69.2 1.3 fusion.15
  70.5 1.9 %fusion.10 = bf16[512,1024]{1,0:T(8,128)(2,1)S(1)} fusion(bf16[4,128,1024]{2,1,0:T(8,128)(2,1)S(1)} %copy-done.5, f32[512,1024]{1,0:T(8,128)S(1)} %fusion.15, f32[512,1024]{1,0:T(8,128)S(1)} %fusion.13, bf16[512,1024]{1,0:T(8,128)(2,1)S(1)} %bitcast.142, bf16[3,1024,1024]{2,1,0:T(8,128)(2,1)S(1)} %bitcast.146), kind=kOutput, calls=%fused_computation.22 | convolution fusion | flops 1080033280 | bytes 9437184 | tf_op jit(solution)/shard_map/dot_general | solution.py:265
  72.4 1.8 %collective-permute-start.7 = (bf16[4,128,1024]{2,1,0:T(8,128)(2,1)S(1)}, bf16[4,128,1024]{2,1,0:T(8,128)(2,1)S(1)}, u32[]{:S(2)}, u32[]{:S(2)}) collective-permute-start(bf16[4,128,1024]{2,1,0:T(8,128)(2,1)S(1)} %bitcast.140), channel_id=1, source_target_pairs={{0,1},{1,0},{2,3},{3,2},{4,5},{5,4},{6,7},{7,6},{8,9},{9,8},{10,11... | collective-permute-start | bytes 3145736 | tf_op jit(solution)/shard_map/ppermute | solution.py:193
  74.2 1.2 fusion.21
  75.4 1.3 fusion.23
  76.8 1.3 fusion.25
  78.2 1.3 fusion.27
  79.5 1.3 fusion.29
  80.8 1.3 fusion.31.q_ref
  82.2 2.6 %copy-done = bf16[6,512,1024]{2,1,0:T(8,128)(2,1)} copy-done((bf16[6,512,1024]{2,1,0:T(8,128)(2,1)}, bf16[6,512,1024]{2,1,0:T(8,128)(2,1)S(1)}, u32[]{:S(2)}) %copy-start) | copy-done | bytes 6291480
  84.8 79.9 %reduce_filters.1 = f32[6,128,1024]{2,1,0:T(8,128)S(1)} custom-call(bf16[6,512,1024]{2,1,0:T(8,128)(2,1)} %copy-done), custom_call_target="tpu_custom_call" | custom-call | tf_op jit(solution)/shard_map/reduce_filters/pallas_call | solution.py:152
  164.7 2.1 %slice_bitcast_fusion = (f32[128,3,1024]{2,0,1:T(8,128)}, f32[128,3,1024]{2,0,1:T(8,128)}) fusion(f32[2,128,3,1024]{3,1,2,0:T(8,128)S(1)} %bitcast.134), kind=kLoop, calls=%fused_computation.36 | loop fusion | bytes 6291456 | tf_op jit(solution)/shard_map/squeeze | solution.py:276
  (48 shorter events, 2.2 us)
Async XLA Ops:
  4.7 15.2 %all-to-all-start = ((s32[8,1,64]{2,1,0:T(1,128)}), s32[8,1,64]{2,1,0:T(1,128)S(1)}, u32[]{:S(2)}, u32[]{:S(2)}) async-start(s32[8,1,64]{2,1,0:T(1,128)} %all_to_all.9), calls=%async_computation | async-start | bytes 8192 | tf_op jit(solution)/shard_map/all_to_all | solution.py:235
  16.4 8.7 %copy-start.4 = (bf16[4,128,1024]{2,1,0:T(8,128)(2,1)S(1)}, bf16[4,128,1024]{2,1,0:T(8,128)(2,1)}, u32[]{:S(2)}) copy-start(bf16[4,128,1024]{2,1,0:T(8,128)(2,1)} %param.10) | copy-start | bytes 3145732
  19.8 5.9 %copy-start.3 = (bf16[4,128,1024]{2,1,0:T(8,128)(2,1)S(1)}, bf16[4,128,1024]{2,1,0:T(8,128)(2,1)}, u32[]{:S(2)}) copy-start(bf16[4,128,1024]{2,1,0:T(8,128)(2,1)} %param.9) | copy-start | bytes 3145732
  19.8 37.6 %all-to-all-start.1 = ((bf16[8,64,1024]{2,1,0:T(8,128)(2,1)}), bf16[8,64,1024]{2,1,0:T(8,128)(2,1)}, u32[]{:S(2)}, u32[]{:S(2)}) async-start(bf16[8,64,1024]{2,1,0:T(8,128)(2,1)} %bitcast.10), calls=%async_computation.1 | async-start | bytes 2097152 | tf_op jit(solution)/shard_map/all_to_all | solution.py:228
  32.6 7.6 %copy-start.1 = (bf16[4,128,4,1,128]{4,3,2,1,0:T(2,128)(2,1)S(1)}, bf16[4,128,4,1,128]{4,3,2,1,0:T(2,128)(2,1)}, u32[]{:S(2)}) copy-start(bf16[4,128,4,1,128]{4,3,2,1,0:T(2,128)(2,1)} %get-tuple-element.24) | copy-start | bytes 1572868
  36.2 5.5 %collective-permute-start = (bf16[4,128,512]{1,2,0:T(8,128)(2,1)}, bf16[4,128,512]{1,2,0:T(8,128)(2,1)}, u32[]{:S(2)}, u32[]{:S(2)}) collective-permute-start(bf16[4,128,512]{1,2,0:T(8,128)(2,1)} %bitcast.1), channel_id=1, source_target_pairs={{0,1},{1,0},{2,3},{3,2},{4,5},{5,4},{6,7},{7,6},{8,9},{9,8},{10,11... | collective-permute-start | bytes 1572872 | tf_op jit(solution)/shard_map/ppermute | solution.py:193
  40.2 2.8 %collective-permute-start.1 = (bf16[4,128,512]{1,2,0:T(8,128)(2,1)}, bf16[4,128,512]{1,2,0:T(8,128)(2,1)S(1)}, u32[]{:S(2)}, u32[]{:S(2)}) collective-permute-start(bf16[4,128,512]{1,2,0:T(8,128)(2,1)} %bitcast.4), channel_id=1, source_target_pairs={{0,1},{1,0},{2,3},{3,2},{4,5},{5,4},{6,7},{7,6},{8,9},{9,8},{10,11... | collective-permute-start | bytes 1572872 | tf_op jit(solution)/shard_map/ppermute | solution.py:193
  46.2 7.0 %collective-permute-start.2 = (bf16[2,4,1,512]{3,1,2,0:T(4,128)(2,1)S(1)}, bf16[2,4,1,512]{3,1,2,0:T(4,128)(2,1)S(1)}, u32[]{:S(2)}, u32[]{:S(2)}) collective-permute-start(bf16[2,4,1,512]{3,1,2,0:T(4,128)(2,1)S(1)} %copy.38), channel_id=1, source_target_pairs={{0,2},{1,3},{2,4},{3,5},{4,6},{5,7},{8,10},{9,11},{10,12},{11,13},... | collective-permute-start | bytes 24584 | tf_op jit(solution)/shard_map/ppermute | solution.py:209
  50.5 5.5 %collective-permute-start.3 = (bf16[2,4,1,512]{3,1,2,0:T(4,128)(2,1)S(1)}, bf16[2,4,1,512]{3,1,2,0:T(4,128)(2,1)S(1)}, u32[]{:S(2)}, u32[]{:S(2)}) collective-permute-start(bf16[2,4,1,512]{3,1,2,0:T(4,128)(2,1)S(1)} %copy.39), channel_id=1, source_target_pairs={{2,0},{3,1},{4,2},{5,3},{6,4},{7,5},{10,8},{11,9},{12,10},{13,11},... | collective-permute-start | bytes 24584 | tf_op jit(solution)/shard_map/ppermute | solution.py:210
  57.5 2.2 %copy-start.2 = (bf16[2,4,1,512]{2,3,1,0:T(8,128)(2,1)S(1)}, bf16[2,4,1,512]{2,3,1,0:T(8,128)(2,1)}, u32[]{:S(2)}) copy-start(bf16[2,4,1,512]{2,3,1,0:T(8,128)(2,1)} %copy.41) | copy-start | bytes 24580
  57.5 9.4 %slice-start = ((s8[6291456]{0:T(1024)(128)(4,1)}), s8[4194304]{0:T(1024)(128)(4,1)S(1)}, s32[]{:S(2)}) async-start(s8[6291456]{0:T(1024)(128)(4,1)} %bitcast.145), calls=%async_computation.2 | async-start | bytes 8388608
  59.6 7.3 %slice-start.1 = ((s8[6291456]{0:T(1024)(128)(4,1)}), s8[2097152]{0:T(1024)(128)(4,1)S(1)}, s32[]{:S(2)}) async-start(s8[6291456]{0:T(1024)(128)(4,1)} %bitcast.145), calls=%async_computation.3 | async-start | bytes 4194304
  59.6 8.6 %collective-permute-start.4 = (bf16[4,128,1024]{2,1,0:T(8,128)(2,1)S(1)}, bf16[4,128,1024]{2,1,0:T(8,128)(2,1)S(1)}, u32[]{:S(2)}, u32[]{:S(2)}) collective-permute-start(bf16[4,128,1024]{2,1,0:T(8,128)(2,1)S(1)} %bitcast.137), channel_id=1, source_target_pairs={{0,1},{1,0},{2,3},{3,2},{4,5},{5,4},{6,7},{7,6},{8,9},{9,8},{10,11... | collective-permute-start | bytes 3145736 | tf_op jit(solution)/shard_map/ppermute | solution.py:193
  62.5 5.7 %collective-permute-start.5 = (bf16[4,1,1024]{2,1,0:T(2,128)(2,1)S(1)}, bf16[4,1,1024]{2,1,0:T(2,128)(2,1)S(1)}, u32[]{:S(2)}, u32[]{:S(2)}) collective-permute-start(bf16[4,1,1024]{2,1,0:T(2,128)(2,1)S(1)} %get-tuple-element.16), channel_id=1, source_target_pairs={{1,0},{2,1},{3,2},{4,3},{5,4},{6,5},{7,6},{9,8},{10,9},{11,10},{12... | collective-permute-start | bytes 24584 | tf_op jit(solution)/shard_map/ppermute | solution.py:248
  63.8 4.4 %collective-permute-start.6 = (bf16[4,1,1024]{2,1,0:T(2,128)(2,1)S(1)}, bf16[4,1,1024]{2,1,0:T(2,128)(2,1)S(1)}, u32[]{:S(2)}, u32[]{:S(2)}) collective-permute-start(bf16[4,1,1024]{2,1,0:T(2,128)(2,1)S(1)} %get-tuple-element.17), channel_id=1, source_target_pairs={{0,1},{1,2},{2,3},{3,4},{4,5},{5,6},{6,7},{8,9},{9,10},{10,11},{11... | collective-permute-start | bytes 24584 | tf_op jit(solution)/shard_map/ppermute | solution.py:247
  69.2 1.3 copy-start.5
  72.4 5.7 %collective-permute-start.7 = (bf16[4,128,1024]{2,1,0:T(8,128)(2,1)S(1)}, bf16[4,128,1024]{2,1,0:T(8,128)(2,1)S(1)}, u32[]{:S(2)}, u32[]{:S(2)}) collective-permute-start(bf16[4,128,1024]{2,1,0:T(8,128)(2,1)S(1)} %bitcast.140), channel_id=1, source_target_pairs={{0,1},{1,0},{2,3},{3,2},{4,5},{5,4},{6,7},{7,6},{8,9},{9,8},{10,11... | collective-permute-start | bytes 3145736 | tf_op jit(solution)/shard_map/ppermute | solution.py:193
  82.1 2.6 %copy-start = (bf16[6,512,1024]{2,1,0:T(8,128)(2,1)}, bf16[6,512,1024]{2,1,0:T(8,128)(2,1)S(1)}, u32[]{:S(2)}) copy-start(bf16[6,512,1024]{2,1,0:T(8,128)(2,1)S(1)} %fusion.31.q_ref) | copy-start | bytes 18874372

commit v2 on v1

v2 whole, which is shorter than its diff:
```python
import functools

import jax
import jax.numpy as jnp
from jax import lax
from jax.experimental import pallas as pl
from jax.experimental.pallas import tpu as pltpu
from jax.sharding import PartitionSpec as P

MESH = pl.DeviceIdType.MESH
UNITS = 2
VMEM_LIMIT = 60 * 1024 * 1024


def silu_slope(values):
    sigma = jax.nn.sigmoid(values)
    return sigma * (1.0 + values * (1.0 - sigma))


def row_of(ref, index, *lead):
    group = ref[(*lead, pl.ds(index // 16 * 16, 16), slice(None))].astype(jnp.float32)
    return group[index % 16 : index % 16 + 1, :]


def pack_rows(row_list):
    width = row_list[0].shape[1]
    place = lax.broadcasted_iota(jnp.int32, (16, width), 0)
    packed = jnp.zeros((16, width), jnp.float32)
    for i, row in enumerate(row_list):
        packed = jnp.where(place == i, row, packed)
    return packed.astype(jnp.bfloat16)


def moved(block, edge, amount):
    count = block.shape[0]
    place = lax.broadcasted_iota(jnp.int32, block.shape, 0)
    if amount == 1:
        return jnp.where(place == 0, edge, pltpu.roll(block, 1, 0))
    return jnp.where(place == count - 1, edge, pltpu.roll(block, count - 1, 0))


def whole_kernel(tm, steps, rows, cols, videos, snips, cap, bin_ref, weight_ref, index_ref, feat_ref,
                 pre_ref, pre_lhs_ref, filt_hbm, out_ref, filt, tap_rows, srow, sidx, grow, gidx, act, lhs, win,
                 edge_out, edge_in, gs, gp, gmove, gedge_out, gedge_in, acc, q_ref,
                 r1, s1, r2, t2, r3, g4, r4,
                 p1_s, p1_r, p2_s, p2_r, p3_s, p3_r, p4_s, p4_r,
                 row_s, row_r, idx_s, idx_r, lhs_s, lhs_r, edge_s, edge_r, g_s, g_r, ge_s, ge_r, filt_sem):
    depth = tm // 2
    bf, f32 = jnp.bfloat16, jnp.float32
    own = videos * snips
    bins = bin_ref.shape[0]
    taps = 2 * bins
    chip = depth * rows
    aligned = rows % 128 == 0
    pack = 128 // cap
    blocks = depth if aligned else 1
    width = chip // blocks
    video = lax.axis_index("video")
    here = lax.axis_index("tm")
    x, y = lax.rem(video, 2), video // 2
    core, z = lax.rem(here, 2), here // 2
    sibling = z * 2 + 1 - core
    flip_x = y * 2 + (1 - x)
    flip_y = (1 - y) * 2 + x
    flip_xy = (1 - y) * 2 + (1 - x)
    others = (flip_x, flip_y, flip_xy)
    other_bits = ((1 - x, y), (x, 1 - y), (1 - x, 1 - y))
    half, quarter = cols // 4, cols // 8

    def z_slot_row(peer_z):
        return pl.multiple_of(peer_z * rows, rows)

    filt_copy = pltpu.make_async_copy(filt_hbm, filt, filt_sem)
    filt_copy.start()
    barrier = pltpu.get_barrier_semaphore()
    for v in others:
        pl.semaphore_signal(barrier, inc=1, device_id={"video": v}, device_id_type=MESH)

    @pl.loop(1, tm)
    def _(j):
        pl.semaphore_signal(barrier, inc=1, device_id={"tm": lax.rem(here + j, tm)}, device_id_type=MESH)

    for j in range(2):
        tap_rows[j * bins : (j + 1) * bins, :] = (
            weight_ref[:, j : j + 1] * bin_ref[...].astype(f32)).astype(bf)
    index = index_ref[...]
    target = index // snips
    lane = lax.broadcasted_iota(jnp.int32, (1, taps), 1)
    video_of = lax.rem(lane, bins) // (bins // videos)
    place8 = lax.broadcasted_iota(jnp.int32, (tm, taps), 0)
    hits = (place8 == target).astype(f32)
    upper = (lax.broadcasted_iota(jnp.int32, (taps, taps), 0)
             < lax.broadcasted_iota(jnp.int32, (taps, taps), 1)).astype(f32).astype(bf)
    earlier = jnp.dot(hits.astype(bf), upper, preferred_element_type=f32)
    position = jnp.sum(earlier * hits, axis=0, keepdims=True).astype(jnp.int32)
    slot = target * cap + position
    group = min(512, tm * cap)
    for g in range(tm * cap // group):
        match = (slot - g * group == lax.broadcasted_iota(jnp.int32, (group, taps), 0)).astype(f32).astype(bf)
        srow[g * group : (g + 1) * group, :] = jnp.dot(
            match, tap_rows[...], preferred_element_type=f32).astype(bf)
    place = lax.broadcasted_iota(jnp.int32, (8, taps), 0)
    coded = jnp.where(place == 0, (video_of + 1).astype(f32), 0.0)
    coded = jnp.where(place == 1, (index - target * snips).astype(f32), coded).astype(bf)

    @pl.loop(0, tm)
    def _(d):
        offset = lax.rem(lax.rem(d - here + tm, tm), pack) * cap
        wide = (target - d) * 4096 + position + offset
        match = (wide == lax.broadcasted_iota(jnp.int32, (128, taps), 0)).astype(f32).astype(bf)
        sidx[d] = lax.dot_general(coded, match, (((1,), (1,)), ((), ())), preferred_element_type=f32)

    def row_copy(j):
        peer = lax.rem(here + j, tm)
        return pltpu.make_async_remote_copy(
            src_ref=srow.at[pl.ds(pl.multiple_of(peer * cap, cap), cap)], dst_ref=grow.at[j],
            send_sem=row_s.at[j], recv_sem=row_r.at[j], device_id={"tm": peer}, device_id_type=MESH)

    def idx_copy(j):
        peer = lax.rem(here + j, tm)
        return pltpu.make_async_remote_copy(
            src_ref=sidx.at[peer], dst_ref=gidx.at[j],
            send_sem=idx_s.at[j], recv_sem=idx_r.at[j], device_id={"tm": peer}, device_id_type=MESH)

    grow[0] = srow[pl.ds(pl.multiple_of(here * cap, cap), cap), :]
    gidx[0] = sidx[here]
    pl.semaphore_wait(barrier, 3 + tm - 1)

    @pl.loop(1, tm)
    def _(j):
        idx_copy(j).start()
        row_copy(j).start()

    def column_of(b, c):
        start = (b * 2 + c) * rows if aligned else c * chip
        return pl.ds(pl.multiple_of(start, 128), width)

    def lhs_copy(kind, b):
        source = (feat_ref, act)[kind]
        return pltpu.make_async_remote_copy(
            src_ref=source.at[:, column_of(b, 1 - core)],
            dst_ref=lhs.at[kind, core, :, pl.ds(b * width, width)],
            send_sem=lhs_s.at[kind, b], recv_sem=lhs_r.at[kind, b],
            device_id={"tm": sibling}, device_id_type=MESH)

    for b in range(blocks):
        lhs_copy(0, b).start()

    @pl.loop(0, own // 64)
    def _(r):
        part = pl.ds(pl.multiple_of(r * 64, 64), 64)
        values = pre_lhs_ref[part, :].astype(f32)
        act[part, :] = (values * jax.nn.sigmoid(values)).astype(bf)

    for b in range(blocks):
        lhs_copy(1, b).start()
    for side in range(2):
        at = 0 if side == 0 else snips - 1
        edge_out[side] = pack_rows(
            [row_of(ref, v * snips + at) for ref in (feat_ref, act) for v in range(videos)])
    toward = lax.rem(z + 2 * core - 1 + depth, depth)

    def edge_copy(c):
        return pltpu.make_async_remote_copy(
            src_ref=edge_out.at[core], dst_ref=edge_in.at[1 - core],
            send_sem=edge_s.at[c], recv_sem=edge_r.at[1 - core],
            device_id={"tm": toward * 2 + c}, device_id_type=MESH)

    def edge_arrival(s):
        return pltpu.make_async_remote_copy(
            src_ref=edge_out.at[0], dst_ref=edge_in.at[s],
            send_sem=edge_s.at[0], recv_sem=edge_r.at[s],
            device_id={"tm": sibling}, device_id_type=MESH)

    for c in range(2):
        edge_copy(c).start()
    for kind in range(2):
        for b in range(blocks):
            lhs[kind, core, :, b * width : (b + 1) * width] = (feat_ref, act)[kind][:, column_of(b, core)]
    for s in range(2):
        edge_arrival(s).wait_recv()
    for kind in range(2):
        for b in range(blocks):
            lhs_copy(kind, b).wait_recv()
        for b in range(blocks):
            piece = pl.ds(b * width, width)
            for v in range(videos):
                spot = kind * videos + v
                halves = [lhs[kind, c, v * snips : (v + 1) * snips, piece].astype(f32) for c in range(2)]
                ends = [jnp.where(edge_ok, edge_in[s, :, column_of(b, core)].astype(f32)[spot : spot + 1, :], 0.0)
                        for s, edge_ok in ((0, z > 0), (1, z < depth - 1))]
                for c in range(2):
                    span = pl.ds(c * own + v * snips, snips)
                    prior = ends[0] if c == 0 else halves[0][snips - 1 :, :]
                    later = ends[1] if c == 1 else halves[1][:1, :]
                    win[kind, 0, piece, span] = moved(halves[c], prior, 1).T.astype(bf)
                    win[kind, 1, piece, span] = halves[c].T.astype(bf)
                    win[kind, 2, piece, span] = moved(halves[c], later, -1).T.astype(bf)

    @pl.loop(1, tm)
    def _(j):
        idx_copy(j).wait_recv()
        row_copy(j).wait_recv()

    many = min(8, tm)
    chunk = 256
    for g in range(tm // many):
        pieces = []
        for j in range(g * many, (g + 1) * many, pack):
            both = gidx[j]
            for i in range(1, pack):
                both = both + gidx[j + i]
            code = both[0:1, :] * float(snips) + both[1:2, :] - float(snips)
            spots = lax.broadcasted_iota(jnp.int32, (own, 128), 0).astype(f32)
            pieces.append((spots == code).astype(f32).astype(bf))
        table = jnp.concatenate(pieces, axis=1)
        for n in range(cols // chunk):
            part = slice(n * chunk, (n + 1) * chunk)
            term = jnp.dot(table, grow[g * many : (g + 1) * many, :, part].reshape(many * cap, chunk),
                           preferred_element_type=f32)
            if tm == many:
                gs[core, :, part] = term.astype(bf)
            else:
                acc[:, part] = term if g == 0 else acc[:, part] + term
    if tm != many:
        gs[core] = acc[...].astype(bf)

    def grad_copy(i):
        ref = (gs, gp)[i]
        return pltpu.make_async_remote_copy(
            src_ref=ref.at[core], dst_ref=ref.at[core],
            send_sem=g_s.at[i], recv_sem=g_r.at[i], device_id={"tm": sibling}, device_id_type=MESH)

    grad_copy(0).start()
    gedge_out[...] = pack_rows([
        jnp.where(core == 1, row_of(gs, v * snips + snips - 1, core), row_of(gs, v * snips, core))
        for v in range(videos)])
    gedge_copy = pltpu.make_async_remote_copy(
        src_ref=gedge_out, dst_ref=gedge_in, send_sem=ge_s, recv_sem=ge_r,
        device_id={"tm": toward * 2 + 1 - core}, device_id_type=MESH)
    gedge_copy.start()

    def product(step):
        kind, k = (1, step) if step < 3 else (0, step - 3)
        grads = gs if step < 3 else gp

        @pl.loop(0, cols // chunk)
        def _(n):
            part = pl.ds(pl.multiple_of(n * chunk, chunk), chunk)
            q_ref[step, :, part] = jnp.dot(
                win[kind, k], grads[:, :, part].reshape(2 * own, chunk), preferred_element_type=f32).astype(bf)

    def bits(kind, xb, yb):
        return (xb, yb) if kind == 0 else (yb, xb)

    def first(step, kind):
        u = step * UNITS + kind
        h1, _ = bits(kind, 1 - x, 1 - y)
        col = pl.multiple_of(kind * (cols // 2) + h1 * half, 128)
        return pltpu.make_async_remote_copy(
            src_ref=q_ref.at[step, :, pl.ds(col, half)], dst_ref=r1.at[u],
            send_sem=p1_s.at[u], recv_sem=p1_r.at[u],
            device_id={"video": (flip_x, flip_y)[kind]}, device_id_type=MESH)

    def second(step, kind):
        u = step * UNITS + kind
        _, h2 = bits(kind, 1 - x, 1 - y)
        return pltpu.make_async_remote_copy(
            src_ref=s1.at[u, :, pl.ds(pl.multiple_of(h2 * quarter, 128), quarter)], dst_ref=r2.at[u],
            send_sem=p2_s.at[u], recv_sem=p2_r.at[u],
            device_id={"video": (flip_y, flip_x)[kind]}, device_id_type=MESH)

    def third(step, kind, j):
        u = step * UNITS + kind
        peer = lax.rem(z + 1 + j, depth)
        return pltpu.make_async_remote_copy(
            src_ref=t2.at[u, pl.ds(z_slot_row(peer), rows)], dst_ref=r3.at[u, j],
            send_sem=p3_s.at[u, j], recv_sem=p3_r.at[u, j],
            device_id={"tm": peer * 2 + core}, device_id_type=MESH)

    def fourth(step, kind, j):
        u = step * UNITS + kind
        return pltpu.make_async_remote_copy(
            src_ref=g4.at[u], dst_ref=r4.at[u, j],
            send_sem=p4_s.at[u, j], recv_sem=p4_r.at[u, j],
            device_id={"video": others[j]}, device_id_type=MESH)

    def column(kind, xb, yb):
        h1, h2 = bits(kind, xb, yb)
        return pl.ds(pl.multiple_of(kind * (cols // 2) + h1 * half + h2 * quarter, 128), quarter)


    def ready(step):
        if step == 3:
            grad_copy(1).wait_recv()
        product(step)
        for kind in range(UNITS):
            first(step, kind).start()

    grad_copy(0).wait_recv()
    ready(0)

    gedge_copy.wait_recv()
    outside_ok = jnp.where(core == 1, z < depth - 1, z > 0)
    outside = jnp.where(outside_ok, gedge_in[...].astype(f32), 0.0)
    for v in range(videos):
        mine = gs[core, v * snips : (v + 1) * snips, :].astype(f32)
        far = outside[v : v + 1, :]
        near = jnp.where(core == 1, row_of(gs, v * snips + snips - 1, 1 - core), row_of(gs, v * snips, 1 - core))
        prior = jnp.where(core == 1, near, far)
        later = jnp.where(core == 1, far, near)
        gmove[0, v * snips : (v + 1) * snips, :] = moved(mine, prior, 1).astype(bf)
        gmove[1, v * snips : (v + 1) * snips, :] = moved(mine, later, -1).astype(bf)
    filt_copy.wait()

    @pl.loop(0, cols // chunk)
    def _(n):
        part = pl.ds(pl.multiple_of(n * chunk, chunk), chunk)
        total = jnp.zeros((own, chunk), f32)
        for lag, window in enumerate((gmove[1], gs[core], gmove[0])):
            total = total + lax.dot_general(
                window, filt[lag, part, :], (((1,), (1,)), ((), ())), preferred_element_type=f32)
        gp[core, :, part] = (total * silu_slope(pre_ref[:, part].astype(f32))).astype(bf)

    grad_copy(1).start()
    ready(1)

    for turn in range(steps + 3):
        if turn + 2 < steps:
            ready(turn + 2)
        if turn < steps:
            for kind in range(UNITS):
                u = turn * UNITS + kind
                first(turn, kind).wait_recv()
                h1, _ = bits(kind, x, y)
                col = pl.multiple_of(kind * (cols // 2) + h1 * half, 128)
                s1[u] = (q_ref[turn, :, pl.ds(col, half)].astype(jnp.float32)
                         + r1[u].astype(jnp.float32)).astype(jnp.bfloat16)
                second(turn, kind).start()
        step = turn - 1
        if 0 <= step < steps:
            for kind in range(UNITS):
                u = step * UNITS + kind
                second(step, kind).wait_recv()
                _, h2 = bits(kind, x, y)
                mine = s1[u, :, pl.ds(pl.multiple_of(h2 * quarter, 128), quarter)]
                t2[u] = (mine.astype(jnp.float32) + r2[u].astype(jnp.float32)).astype(jnp.bfloat16)
                for j in range(depth - 1):
                    third(step, kind, j).start()
        step = turn - 2
        if 0 <= step < steps:
            for kind in range(UNITS):
                u = step * UNITS + kind
                total = t2[u, pl.ds(z_slot_row(z), rows)].astype(jnp.float32)
                for j in range(depth - 1):
                    third(step, kind, j).wait_recv()
                    total = total + r3[u, j].astype(jnp.float32)
                g4[u] = total.astype(jnp.bfloat16)
                for j in range(3):
                    fourth(step, kind, j).start()
                out_ref[step, :, column(kind, x, y)] = g4[u].astype(jnp.float32)
        step = turn - 3
        if 0 <= step < steps:
            for kind in range(UNITS):
                u = step * UNITS + kind
                for j in range(3):
                    fourth(step, kind, j).wait_recv()
                    out_ref[step, :, column(kind, *other_bits[j])] = r4[u, j].astype(jnp.float32)

    for step in range(steps):
        for kind in range(UNITS):
            first(step, kind).wait_send()
            second(step, kind).wait_send()
            for j in range(depth - 1):
                third(step, kind, j).wait_send()
            for j in range(3):
                fourth(step, kind, j).wait_send()
    for c in range(2):
        edge_copy(c).wait_send()
    for kind in range(2):
        for b in range(blocks):
            lhs_copy(kind, b).wait_send()
    for i in range(2):
        grad_copy(i).wait_send()
    gedge_copy.wait_send()

    @pl.loop(1, tm)
    def _(j):
        idx_copy(j).wait_send()
        row_copy(j).wait_send()


def on_device(bin_grad, tap_weight, tap_index, features, preact, filter_second):
    video_count, prop_count, bin_count, tap_count = tap_index.shape
    snips, cols = features.shape[1:]
    tm = lax.axis_size("tm")
    depth = tm // 2
    rows = cols // tm
    chip = depth * rows
    own = video_count * snips
    bins = video_count * prop_count * bin_count
    cap = bin_count * tap_count * ((video_count * prop_count + tm - 1) // tm)
    steps = 6
    n = steps * UNITS
    half, quarter = cols // 4, cols // 8
    blocks = depth if rows % 128 == 0 else 1
    bf, f32 = jnp.bfloat16, jnp.float32
    dma = pltpu.SemaphoreType.DMA
    vmem = pl.BlockSpec(memory_space=pltpu.VMEM)
    features = features.reshape(own, cols)
    preact = preact.reshape(own, cols)

    def by_core(values):
        if rows % 128 == 0:
            return values
        return values.reshape(own, depth, 2, rows).swapaxes(1, 2).reshape(own, cols)

    sums = pl.pallas_call(
        functools.partial(whole_kernel, tm, steps, rows, cols, video_count, snips, cap),
        out_shape=jax.ShapeDtypeStruct((steps, rows, cols), f32),
        in_specs=[vmem] * 6 + [pl.BlockSpec(memory_space=pl.ANY)],
        out_specs=vmem,
        scratch_shapes=[
            pltpu.VMEM(filter_second.shape, bf),
            pltpu.VMEM((2 * bins, cols), bf),
            pltpu.VMEM((tm * cap, cols), bf),
            pltpu.VMEM((tm, 8, 128), f32),
            pltpu.VMEM((tm, cap, cols), bf),
            pltpu.VMEM((tm, 8, 128), f32),
            pltpu.VMEM((own, cols), bf),
            pltpu.VMEM((2, 2, own, chip), bf),
            pltpu.VMEM((2, 3, chip, 2 * own), bf),
            pltpu.VMEM((2, 16, cols), bf),
            pltpu.VMEM((2, 16, cols), bf),
            pltpu.VMEM((2, own, cols), bf),
            pltpu.VMEM((2, own, cols), bf),
            pltpu.VMEM((2, own, cols), bf),
            pltpu.VMEM((16, cols), bf),
            pltpu.VMEM((16, cols), bf),
            pltpu.VMEM((own, cols) if tm > 8 else (8, 128), f32),
            pltpu.VMEM((steps, chip, cols), bf),
            pltpu.VMEM((n, chip, half), bf),
            pltpu.VMEM((n, chip, half), bf),
            pltpu.VMEM((n, chip, quarter), bf),
            pltpu.VMEM((n, chip, quarter), bf),
            pltpu.VMEM((n, depth - 1, rows, quarter), bf),
            pltpu.VMEM((n, rows, quarter), bf),
            pltpu.VMEM((n, 3, rows, quarter), bf),
            dma((n,)), dma((n,)), dma((n,)), dma((n,)),
            dma((n, depth - 1)), dma((n, depth - 1)), dma((n, 3)), dma((n, 3)),
            dma((tm,)), dma((tm,)), dma((tm,)), dma((tm,)),
            dma((2, blocks)), dma((2, blocks)), dma((2,)), dma((2,)),
            dma((2,)), dma((2,)), dma, dma, dma,
        ],
        compiler_params=pltpu.CompilerParams(
            collective_id=0, has_side_effects=True, vmem_limit_bytes=VMEM_LIMIT
        ),
        name="filter_grads",
    )(
        bin_grad.reshape(bins, cols),
        tap_weight.reshape(bins, tap_count),
        tap_index.reshape(bins, tap_count).T.reshape(1, tap_count * bins),
        by_core(features),
        preact,
        by_core(preact),
        filter_second,
    )
    out = sums.reshape(2, 3, rows, cols).transpose(0, 2, 1, 3)
    return (out[1], out[0])


def solution(mesh):
    return jax.shard_map(
        on_device,
        mesh=mesh,
        in_specs=(
            P("video", "tm", None, None),
            P("video", "tm", None, None),
            P("video", "tm", None, None),
            P("video", "tm", None),
            P("video", "tm", None),
            P(),
        ),
        out_specs=(P("tm", None, None), P("tm", None, None)),
        check_vma=False,
    )
```

time: 167 us -> 124 us (0.74)
  Pallas kernels: 79.9 us -> 116 us
  local copies, waits for them, and re-layouts: 32.1 us -> 6.89 us
  starting transfers between devices: 23.6 us -> 0 us
  matrix products: 17.7 us -> 0 us
  other arithmetic: 10.1 us -> 0 us
  waiting for transfers between devices: 2.31 us -> 0 us
    pallas_call x1, Pallas kernels: 79.9 us -> 116 us  [on_device(): pl.pallas_call(functools.partial(whole_kernel, tm, steps, rows, cols, vid...]
    dot_general x11 -> x0, matrix products: 17.7 us -> none  [the longest x6 7.75 us: filter_terms(): lax.dot_general(padded[:, k:k + 2 * snip_count].reshape(-1, depth * rows)...]
    ppermute x8 -> x0, starting transfers between devices: 12.1 us -> none  [the longest x1 3.92 us: on_device(): before = lax.ppermute(lhs[:, :, -1:], 'tm', up)]
    all_to_all x2 -> x0, starting transfers between devices: 11.6 us -> none  [the longest x1 6.33 us: on_device(): lax.all_to_all(send_index.reshape(peers, capacity), 'tm', split_axis=0, c...]
    unnamed x21 -> x3, local copies, waits for them, and re-layouts: 12.1 us -> 2.84 us
    dynamic_slice x1 -> x0, local copies, waits for them, and re-layouts: 5.34 us -> none  [chip_lhs(): lax.dynamic_index_in_dim(split, c, 3, keepdims=False)]
    mul x3 -> x0, local copies, waits for them, and re-layouts: 4.53 us -> none  [on_device(): tap_weight[..., None] * bin_grad[:, :, :, None, :].astype(jnp.float32)]
    concatenate x2 -> x0, other arithmetic: 3.46 us -> none  [the longest x1 2.46 us: on_device(): lhs = jnp.concatenate([before, lhs, after], axis=2)]
  transfers between devices with their start and end apart: 10 -> 0, of which waited for: 1 -> 0; matrix products, arithmetic and copies ran while one was open for 24% -> 0% of each run, Pallas kernels for 0% -> 0%
where the time goes in v2:
time: 124 us; the launch traced here: 123 us
  Pallas kernels  116 us (94%)
  local copies, waits for them, and re-layouts  6.89 us (6%)
    pallas_call x1, Pallas kernels, on_device(): pl.pallas_call(functools.partial(whole_kernel, tm, steps, rows, cols, vid...  116 us
    squeeze x1, local copies, waits for them, and re-layouts, on_device(): return (out[1], out[0])  3.96 us
    unnamed x3, local copies, waits for them, and re-layouts  2.84 us

profile of v2, /device:TPU:0, one launch (start us, length us, event | category | flops | bytes accessed | tf_op | source)
XLA Modules:
  0.0 123.3 jit_solution(7601368998089632958)
XLA Ops:
  0.6 0.7 copy.10
  1.4 0.1 reshape.27
  1.4 0.6 copy.11
  2.0 1.5 %copy.9 = f32[4,4,16,2]{3,2,1,0:T(8,128)} copy(f32[4,4,16,2]{2,3,1,0:T(2,128)} %param.7) | data formatting | bytes 4096 | tf_op args[1]
  3.6 115.8 %filter_grads.1 = f32[6,128,1024]{2,1,0:T(8,128)} custom-call(bf16[256,1024]{1,0:T(8,128)(2,1)} %bitcast.22, f32[256,2]{1,0:T(8,128)} %bitcast.21, s32[1,512]{1,0:T(1,128)} %bitcast.24, bf16[512,1024]{1,0:T(8,128)(2,1)} %bitcast.20, bf16[512,1024]{1,0:T(8,128)(2,1)} %bitcast.18, bf16[512,1024]{1,0:T(8,128)(2,1)} %bitcast.19, bf16[3,1024,1024]{2,1,0:T(8,128)(2,1)} %filt_hbm.1), custom_call_target="tpu_custom_call" | custom-call | tf_op jit(solution)/shard_map/filter_grads/pallas_call | solution.py:418
  119.4 4.0 %slice_bitcast_fusion = (f32[128,3,1024]{2,0,1:T(8,128)}, f32[128,3,1024]{2,0,1:T(8,128)}) fusion(f32[2,128,3,1024]{3,1,2,0:T(8,128)} %bitcast.17), kind=kLoop, calls=%fused_computation | loop fusion | bytes 6291456 | tf_op jit(solution)/shard_map/squeeze | solution.py:469

commit v3 on v2

--- a/solution.py
+++ b/solution.py
@@ -42,7 +42,7 @@
 def whole_kernel(tm, steps, rows, cols, videos, snips, cap, bin_ref, weight_ref, index_ref, feat_ref,
                  pre_ref, pre_lhs_ref, filt_hbm, out_ref, filt, tap_rows, srow, sidx, grow, gidx, act, lhs, win,
                  edge_out, edge_in, gs, gp, gmove, gedge_out, gedge_in, acc, q_ref,
-                 r1, s1, r2, t2, r3, g4, r4,
+                 r1, s1, r2, t2, r3, rz, zs, z_s, z_r,
                  p1_s, p1_r, p2_s, p2_r, p3_s, p3_r, p4_s, p4_r,
                  row_s, row_r, idx_s, idx_r, lhs_s, lhs_r, edge_s, edge_r, g_s, g_r, ge_s, ge_r, filt_sem):
     depth = tm // 2
@@ -64,7 +64,6 @@
     flip_y = (1 - y) * 2 + x
     flip_xy = (1 - y) * 2 + (1 - x)
     others = (flip_x, flip_y, flip_xy)
-    other_bits = ((1 - x, y), (x, 1 - y), (1 - x, 1 - y))
     half, quarter = cols // 4, cols // 8
 
     def z_slot_row(peer_z):
@@ -250,23 +249,39 @@
             q_ref[step, :, part] = jnp.dot(
                 win[kind, k], grads[:, :, part].reshape(2 * own, chunk), preferred_element_type=f32).astype(bf)
 
+
     def bits(kind, xb, yb):
         return (xb, yb) if kind == 0 else (yb, xb)
+
+    def height(step):
+        return rows if step == 0 else chip
+
+    def z_copy(j):
+        peer = lax.rem(z + 1 + j, depth)
+        return pltpu.make_async_remote_copy(
+            src_ref=q_ref.at[0, pl.ds(z_slot_row(peer), rows)], dst_ref=rz.at[j],
+            send_sem=z_s.at[j], recv_sem=z_r.at[j],
+            device_id={"tm": peer * 2 + core}, device_id_type=MESH)
+
+    def half_of(kind, h1):
+        return pl.ds(pl.multiple_of(kind * (cols // 2) + h1 * half, 128), half)
 
     def first(step, kind):
         u = step * UNITS + kind
         h1, _ = bits(kind, 1 - x, 1 - y)
-        col = pl.multiple_of(kind * (cols // 2) + h1 * half, 128)
-        return pltpu.make_async_remote_copy(
-            src_ref=q_ref.at[step, :, pl.ds(col, half)], dst_ref=r1.at[u],
+        source = zs.at[:, half_of(kind, h1)] if step == 0 else q_ref.at[step, :, half_of(kind, h1)]
+        return pltpu.make_async_remote_copy(
+            src_ref=source, dst_ref=r1.at[u, pl.ds(0, height(step))],
             send_sem=p1_s.at[u], recv_sem=p1_r.at[u],
             device_id={"video": (flip_x, flip_y)[kind]}, device_id_type=MESH)
 
     def second(step, kind):
         u = step * UNITS + kind
         _, h2 = bits(kind, 1 - x, 1 - y)
-        return pltpu.make_async_remote_copy(
-            src_ref=s1.at[u, :, pl.ds(pl.multiple_of(h2 * quarter, 128), quarter)], dst_ref=r2.at[u],
+        tall = pl.ds(0, height(step))
+        return pltpu.make_async_remote_copy(
+            src_ref=s1.at[u, tall, pl.ds(pl.multiple_of(h2 * quarter, 128), quarter)],
+            dst_ref=r2.at[u, tall],
             send_sem=p2_s.at[u], recv_sem=p2_r.at[u],
             device_id={"video": (flip_y, flip_x)[kind]}, device_id_type=MESH)
 
@@ -278,27 +293,58 @@
             send_sem=p3_s.at[u, j], recv_sem=p3_r.at[u, j],
             device_id={"tm": peer * 2 + core}, device_id_type=MESH)
 
-    def fourth(step, kind, j):
-        u = step * UNITS + kind
-        return pltpu.make_async_remote_copy(
-            src_ref=g4.at[u], dst_ref=r4.at[u, j],
-            send_sem=p4_s.at[u, j], recv_sem=p4_r.at[u, j],
-            device_id={"video": others[j]}, device_id_type=MESH)
-
     def column(kind, xb, yb):
         h1, h2 = bits(kind, xb, yb)
         return pl.ds(pl.multiple_of(kind * (cols // 2) + h1 * half + h2 * quarter, 128), quarter)
 
+    def fourth(step, kind, j):
+        u = step * UNITS + kind
+        mine = out_ref.at[step, :, column(kind, x, y)]
+        return pltpu.make_async_remote_copy(
+            src_ref=mine, dst_ref=mine,
+            send_sem=p4_s.at[u, j], recv_sem=p4_r.at[u, j],
+            device_id={"video": others[j]}, device_id_type=MESH)
+
+    def end_first(step, kind):
+        u = step * UNITS + kind
+        first(step, kind).wait_recv()
+        h1, _ = bits(kind, x, y)
+        mine = zs[:, half_of(kind, h1)] if step == 0 else q_ref[step, :, half_of(kind, h1)]
+        tall = height(step)
+        s1[u, :tall] = (mine.astype(f32) + r1[u, :tall].astype(f32)).astype(bf)
+        second(step, kind).start()
+
+    def second_sum(step, kind):
+        u = step * UNITS + kind
+        second(step, kind).wait_recv()
+        _, h2 = bits(kind, x, y)
+        tall = height(step)
+        mine = s1[u, :tall, pl.ds(pl.multiple_of(h2 * quarter, 128), quarter)]
+        return mine.astype(f32) + r2[u, :tall].astype(f32)
+
+    def spread(step, kind, total):
+        out_ref[step, :, column(kind, x, y)] = total.astype(bf)
+        for j in range(3):
+            fourth(step, kind, j).start()
+
+    def end_fourth(step, kind):
+        for j in range(3):
+            fourth(step, kind, j).wait_recv()
 
     def ready(step):
         if step == 3:
             grad_copy(1).wait_recv()
         product(step)
-        for kind in range(UNITS):
-            first(step, kind).start()
+        if step == 0:
+            for j in range(depth - 1):
+                z_copy(j).start()
+        else:
+            for kind in range(UNITS):
+                first(step, kind).start()
 
     grad_copy(0).wait_recv()
     ready(0)
+    ready(1)
 
     gedge_copy.wait_recv()
     outside_ok = jnp.where(core == 1, z < depth - 1, z > 0)
@@ -323,56 +369,63 @@
         gp[core, :, part] = (total * silu_slope(pre_ref[:, part].astype(f32))).astype(bf)
 
     grad_copy(1).start()
-    ready(1)
-
-    for turn in range(steps + 3):
-        if turn + 2 < steps:
-            ready(turn + 2)
-        if turn < steps:
-            for kind in range(UNITS):
-                u = turn * UNITS + kind
-                first(turn, kind).wait_recv()
-                h1, _ = bits(kind, x, y)
-                col = pl.multiple_of(kind * (cols // 2) + h1 * half, 128)
-                s1[u] = (q_ref[turn, :, pl.ds(col, half)].astype(jnp.float32)
-                         + r1[u].astype(jnp.float32)).astype(jnp.bfloat16)
-                second(turn, kind).start()
-        step = turn - 1
-        if 0 <= step < steps:
-            for kind in range(UNITS):
-                u = step * UNITS + kind
-                second(step, kind).wait_recv()
-                _, h2 = bits(kind, x, y)
-                mine = s1[u, :, pl.ds(pl.multiple_of(h2 * quarter, 128), quarter)]
-                t2[u] = (mine.astype(jnp.float32) + r2[u].astype(jnp.float32)).astype(jnp.bfloat16)
+    ready(2)
+
+
+    kinds = range(UNITS)
+    for turn in range(steps + 2):
+        if turn + 3 < steps:
+            ready(turn + 3)
+        if turn == 2:
+            total = q_ref[0, pl.ds(z_slot_row(z), rows)].astype(f32)
+            for j in range(depth - 1):
+                z_copy(j).wait_recv()
+                total = total + rz[j].astype(f32)
+            zs[...] = total.astype(bf)
+            for kind in kinds:
+                first(0, kind).start()
+        if turn == 3:
+            for kind in kinds:
+                end_first(0, kind)
+        if turn == 4:
+            for kind in kinds:
+                spread(0, kind, second_sum(0, kind))
+        if turn == 5:
+            for kind in kinds:
+                end_fourth(0, kind)
+        step = turn + 1
+        if 1 <= step < steps:
+            for kind in kinds:
+                end_first(step, kind)
+        step = turn
+        if 1 <= step < steps:
+            for kind in kinds:
+                t2[step * UNITS + kind] = second_sum(step, kind).astype(bf)
                 for j in range(depth - 1):
                     third(step, kind, j).start()
-        step = turn - 2
-        if 0 <= step < steps:
-            for kind in range(UNITS):
+        step = turn - 1
+        if 1 <= step < steps:
+            for kind in kinds:
                 u = step * UNITS + kind
-                total = t2[u, pl.ds(z_slot_row(z), rows)].astype(jnp.float32)
+                total = t2[u, pl.ds(z_slot_row(z), rows)].astype(f32)
                 for j in range(depth - 1):
                     third(step, kind, j).wait_recv()
-                    total = total + r3[u, j].astype(jnp.float32)
-                g4[u] = total.astype(jnp.bfloat16)
-                for j in range(3):
-                    fourth(step, kind, j).start()
-                out_ref[step, :, column(kind, x, y)] = g4[u].astype(jnp.float32)
-        step = turn - 3
-        if 0 <= step < steps:
-            for kind in range(UNITS):
-                u = step * UNITS + kind
-                for j in range(3):
-                    fourth(step, kind, j).wait_recv()
-                    out_ref[step, :, column(kind, *other_bits[j])] = r4[u, j].astype(jnp.float32)
-
+                    total = total + r3[u, j].astype(f32)
+                spread(step, kind, total)
+        step = turn - 2
+        if 1 <= step < steps:
+            for kind in kinds:
+                end_fourth(step, kind)
+
+    for j in range(depth - 1):
+        z_copy(j).wait_send()
     for step in range(steps):
-        for kind in range(UNITS):
+        for kind in kinds:
             first(step, kind).wait_send()
             second(step, kind).wait_send()
             for j in range(depth - 1):
-                third(step, kind, j).wait_send()
+                if step > 0:
+                    third(step, kind, j).wait_send()
             for j in range(3):
                 fourth(step, kind, j).wait_send()
     for c in range(2):
@@ -415,10 +468,17 @@
             return values
         return values.reshape(own, depth, 2, rows).swapaxes(1, 2).reshape(own, cols)
 
+    aligned = rows % 128 == 0
+    sizes = (tm, steps, rows, cols, video_count, snips, cap)
+
+    def kernel(bin_ref, weight_ref, index_ref, feat_ref, pre_ref, *refs):
+        lhs_refs = (pre_ref,) if aligned else ()
+        whole_kernel(*sizes, bin_ref, weight_ref, index_ref, feat_ref, pre_ref, *lhs_refs, *refs)
+
     sums = pl.pallas_call(
-        functools.partial(whole_kernel, tm, steps, rows, cols, video_count, snips, cap),
-        out_shape=jax.ShapeDtypeStruct((steps, rows, cols), f32),
-        in_specs=[vmem] * 6 + [pl.BlockSpec(memory_space=pl.ANY)],
+        kernel,
+        out_shape=jax.ShapeDtypeStruct((steps, rows, cols), bf),
+        in_specs=[vmem] * (5 if aligned else 6) + [pl.BlockSpec(memory_space=pl.ANY)],
         out_specs=vmem,
         scratch_shapes=[
             pltpu.VMEM(filter_second.shape, bf),
@@ -444,8 +504,9 @@
             pltpu.VMEM((n, chip, quarter), bf),
             pltpu.VMEM((n, chip, quarter), bf),
             pltpu.VMEM((n, depth - 1, rows, quarter), bf),
-            pltpu.VMEM((n, rows, quarter), bf),
-            pltpu.VMEM((n, 3, rows, quarter), bf),
+            pltpu.VMEM((depth - 1, rows, cols), bf),
+            pltpu.VMEM((rows, cols), bf),
+            dma((depth - 1,)), dma((depth - 1,)),
             dma((n,)), dma((n,)), dma((n,)), dma((n,)),
             dma((n, depth - 1)), dma((n, depth - 1)), dma((n, 3)), dma((n, 3)),
             dma((tm,)), dma((tm,)), dma((tm,)), dma((tm,)),
@@ -462,10 +523,10 @@
         tap_index.reshape(bins, tap_count).T.reshape(1, tap_count * bins),
         by_core(features),
         preact,
-        by_core(preact),
+        *(() if aligned else (by_core(preact),)),
         filter_second,
     )
-    out = sums.reshape(2, 3, rows, cols).transpose(0, 2, 1, 3)
+    out = sums.astype(f32).reshape(2, 3, rows, cols).transpose(0, 2, 1, 3)
     return (out[1], out[0])
 
 

time: 124 us -> 120 us (0.968)
  Pallas kernels: 116 us -> 113 us
  local copies, waits for them, and re-layouts: 6.89 us -> 4.82 us
  other arithmetic: 0 us -> 1.79 us
    pallas_call x1, Pallas kernels: 116 us -> 113 us  [on_device(): pl.pallas_call(kernel, out_shape=jax.ShapeDtypeStruct((steps, rows, cols)...]
    squeeze x1, local copies, waits for them, and re-layouts: 3.96 us -> 1.89 us  [on_device(): return (out[1], out[0])]
    transpose x0 -> x1, other arithmetic: none -> 1.79 us  [on_device(): out = sums.astype(f32).reshape(2, 3, rows, cols).transpose(0, 2, 1, 3)]
where the time goes in v3:
time: 120 us
  Pallas kernels  113 us (94%)
  local copies, waits for them, and re-layouts  4.82 us (4%)
  other arithmetic  1.79 us (1%)
    pallas_call x1, Pallas kernels, on_device(): pl.pallas_call(kernel, out_shape=jax.ShapeDtypeStruct((steps, rows, cols)...  113 us
    unnamed x3, local copies, waits for them, and re-layouts  2.84 us

profile of v3, /device:TPU:0, one launch (start us, length us, event | category | flops | bytes accessed | tf_op | source)
XLA Modules:
  0.0 119.8 jit_solution(4161545658630889430)
XLA Ops:
  0.6 0.7 copy.10
  1.4 0.1 reshape.28
  1.4 0.6 copy.11
  2.0 1.5 %copy.9 = f32[4,4,16,2]{3,2,1,0:T(8,128)} copy(f32[4,4,16,2]{2,3,1,0:T(2,128)} %param.7) | data formatting | bytes 4096 | tf_op args[1]
  3.6 112.6 %filter_grads.1 = bf16[6,128,1024]{2,1,0:T(8,128)(2,1)} custom-call(bf16[256,1024]{1,0:T(8,128)(2,1)} %bitcast.22, f32[256,2]{1,0:T(8,128)} %bitcast.21, s32[1,512]{1,0:T(1,128)} %bitcast.23, bf16[512,1024]{1,0:T(8,128)(2,1)} %bitcast.19, bf16[512,1024]{1,0:T(8,128)(2,1)} %bitcast.20, bf16[3,1024,1024]{2,1,0:T(8,128)(2,1)} %refs_0_.1), custom_call_target="tpu_custom_call" | custom-call | tf_op jit(solution)/shard_map/filter_grads/pallas_call | solution.py:478
  116.1 1.8 %convert_bitcast_fusion = f32[2,128,3,1024]{3,1,2,0:T(8,128)S(1)} fusion(bf16[2,3,128,1024]{3,2,1,0:T(8,128)(2,1)} %bitcast.18), kind=kLoop, calls=%fused_computation | loop fusion | flops 786432 | bytes 4718592 | tf_op jit(solution)/shard_map/transpose | solution.py:529
  117.9 1.9 %slice_bitcast_fusion = (f32[128,3,1024]{2,0,1:T(8,128)}, f32[128,3,1024]{2,0,1:T(8,128)}) fusion(f32[2,128,3,1024]{3,1,2,0:T(8,128)S(1)} %convert_bitcast_fusion), kind=kLoop, calls=%fused_computation.1 | loop fusion | bytes 6291456 | tf_op jit(solution)/shard_map/squeeze | solution.py:530

commit v4 on v3

--- a/solution.py
+++ b/solution.py
@@ -40,7 +40,7 @@
 
 
 def whole_kernel(tm, steps, rows, cols, videos, snips, cap, bin_ref, weight_ref, index_ref, feat_ref,
-                 pre_ref, pre_lhs_ref, filt_hbm, out_ref, filt, tap_rows, srow, sidx, grow, gidx, act, lhs, win,
+                 pre_ref, pre_lhs_ref, filt_hbm, out_ref, filt, tap_rows, srow, sidx, grow, gidx, lhs, win,
                  edge_out, edge_in, gs, gp, gmove, gedge_out, gedge_in, acc, q_ref,
                  r1, s1, r2, t2, r3, rz, zs, z_s, z_r,
                  p1_s, p1_r, p2_s, p2_r, p3_s, p3_r, p4_s, p4_r,
@@ -79,6 +79,45 @@
     def _(j):
         pl.semaphore_signal(barrier, inc=1, device_id={"tm": lax.rem(here + j, tm)}, device_id_type=MESH)
 
+    inputs = (feat_ref, pre_lhs_ref)
+
+    def column_of(b, c):
+        start = (b * 2 + c) * rows if aligned else c * chip
+        return pl.ds(pl.multiple_of(start, 128), width)
+
+    def lhs_copy(kind, b):
+        source = inputs[kind]
+        return pltpu.make_async_remote_copy(
+            src_ref=source.at[:, column_of(b, 1 - core)],
+            dst_ref=lhs.at[kind, core, :, pl.ds(b * width, width)],
+            send_sem=lhs_s.at[kind, b], recv_sem=lhs_r.at[kind, b],
+            device_id={"tm": sibling}, device_id_type=MESH)
+
+    for side in range(2):
+        at = 0 if side == 0 else snips - 1
+        edge_out[side] = pack_rows(
+            [row_of(ref, v * snips + at) for ref in inputs for v in range(videos)])
+    toward = lax.rem(z + 2 * core - 1 + depth, depth)
+
+    def edge_copy(c):
+        return pltpu.make_async_remote_copy(
+            src_ref=edge_out.at[core], dst_ref=edge_in.at[1 - core],
+            send_sem=edge_s.at[c], recv_sem=edge_r.at[1 - core],
+            device_id={"tm": toward * 2 + c}, device_id_type=MESH)
+
+    def edge_arrival(s):
+        return pltpu.make_async_remote_copy(
+            src_ref=edge_out.at[0], dst_ref=edge_in.at[s],
+            send_sem=edge_s.at[0], recv_sem=edge_r.at[s],
+            device_id={"tm": sibling}, device_id_type=MESH)
+
+    pl.semaphore_wait(barrier, 3 + tm - 1)
+    for c in range(2):
+        edge_copy(c).start()
+    for kind in range(2):
+        for b in range(blocks):
+            lhs_copy(kind, b).start()
+
     for j in range(2):
         tap_rows[j * bins : (j + 1) * bins, :] = (
             weight_ref[:, j : j + 1] * bin_ref[...].astype(f32)).astype(bf)
@@ -123,59 +162,17 @@
 
     grow[0] = srow[pl.ds(pl.multiple_of(here * cap, cap), cap), :]
     gidx[0] = sidx[here]
-    pl.semaphore_wait(barrier, 3 + tm - 1)
 
     @pl.loop(1, tm)
-    def _(j):
+    def _(i):
+        j = lax.rem(i - 1 + tm // 2 - 1, tm - 1) + 1
         idx_copy(j).start()
         row_copy(j).start()
 
-    def column_of(b, c):
-        start = (b * 2 + c) * rows if aligned else c * chip
-        return pl.ds(pl.multiple_of(start, 128), width)
-
-    def lhs_copy(kind, b):
-        source = (feat_ref, act)[kind]
-        return pltpu.make_async_remote_copy(
-            src_ref=source.at[:, column_of(b, 1 - core)],
-            dst_ref=lhs.at[kind, core, :, pl.ds(b * width, width)],
-            send_sem=lhs_s.at[kind, b], recv_sem=lhs_r.at[kind, b],
-            device_id={"tm": sibling}, device_id_type=MESH)
-
-    for b in range(blocks):
-        lhs_copy(0, b).start()
-
-    @pl.loop(0, own // 64)
-    def _(r):
-        part = pl.ds(pl.multiple_of(r * 64, 64), 64)
-        values = pre_lhs_ref[part, :].astype(f32)
-        act[part, :] = (values * jax.nn.sigmoid(values)).astype(bf)
-
-    for b in range(blocks):
-        lhs_copy(1, b).start()
-    for side in range(2):
-        at = 0 if side == 0 else snips - 1
-        edge_out[side] = pack_rows(
-            [row_of(ref, v * snips + at) for ref in (feat_ref, act) for v in range(videos)])
-    toward = lax.rem(z + 2 * core - 1 + depth, depth)
-
-    def edge_copy(c):
-        return pltpu.make_async_remote_copy(
-            src_ref=edge_out.at[core], dst_ref=edge_in.at[1 - core],
-            send_sem=edge_s.at[c], recv_sem=edge_r.at[1 - core],
-            device_id={"tm": toward * 2 + c}, device_id_type=MESH)
-
-    def edge_arrival(s):
-        return pltpu.make_async_remote_copy(
-            src_ref=edge_out.at[0], dst_ref=edge_in.at[s],
-            send_sem=edge_s.at[0], recv_sem=edge_r.at[s],
-            device_id={"tm": sibling}, device_id_type=MESH)
-
-    for c in range(2):
-        edge_copy(c).start()
     for kind in range(2):
         for b in range(blocks):
-            lhs[kind, core, :, b * width : (b + 1) * width] = (feat_ref, act)[kind][:, column_of(b, core)]
+            lhs[kind, core, :, b * width : (b + 1) * width] = inputs[kind][:, column_of(b, core)]
+    shape_of = (lambda values: values, lambda values: values * jax.nn.sigmoid(values))
     for s in range(2):
         edge_arrival(s).wait_recv()
     for kind in range(2):
@@ -185,8 +182,10 @@
             piece = pl.ds(b * width, width)
             for v in range(videos):
                 spot = kind * videos + v
-                halves = [lhs[kind, c, v * snips : (v + 1) * snips, piece].astype(f32) for c in range(2)]
-                ends = [jnp.where(edge_ok, edge_in[s, :, column_of(b, core)].astype(f32)[spot : spot + 1, :], 0.0)
+                halves = [shape_of[kind](lhs[kind, c, v * snips : (v + 1) * snips, piece].astype(f32))
+                          for c in range(2)]
+                ends = [jnp.where(edge_ok, shape_of[kind](
+                            edge_in[s, :, column_of(b, core)].astype(f32)[spot : spot + 1, :]), 0.0)
                         for s, edge_ok in ((0, z > 0), (1, z < depth - 1))]
                 for c in range(2):
                     span = pl.ds(c * own + v * snips, snips)
@@ -376,7 +375,7 @@
     for turn in range(steps + 2):
         if turn + 3 < steps:
             ready(turn + 3)
-        if turn == 2:
+        if turn == 3:
             total = q_ref[0, pl.ds(z_slot_row(z), rows)].astype(f32)
             for j in range(depth - 1):
                 z_copy(j).wait_recv()
@@ -384,13 +383,13 @@
             zs[...] = total.astype(bf)
             for kind in kinds:
                 first(0, kind).start()
-        if turn == 3:
+        if turn == 4:
             for kind in kinds:
                 end_first(0, kind)
-        if turn == 4:
+        if turn == 5:
             for kind in kinds:
                 spread(0, kind, second_sum(0, kind))
-        if turn == 5:
+        if turn == 6:
             for kind in kinds:
                 end_fourth(0, kind)
         step = turn + 1
@@ -487,7 +486,6 @@
             pltpu.VMEM((tm, 8, 128), f32),
             pltpu.VMEM((tm, cap, cols), bf),
             pltpu.VMEM((tm, 8, 128), f32),
-            pltpu.VMEM((own, cols), bf),
             pltpu.VMEM((2, 2, own, chip), bf),
             pltpu.VMEM((2, 3, chip, 2 * own), bf),
             pltpu.VMEM((2, 16, cols), bf),

time: 120 us -> 115 us (0.958)
  Pallas kernels: 113 us -> 107 us
    pallas_call x1, Pallas kernels: 113 us -> 107 us  [on_device(): pl.pallas_call(kernel, out_shape=jax.ShapeDtypeStruct((steps, rows, cols)...]
where the time goes in v4:
time: 115 us
  Pallas kernels  107 us (93%)
  local copies, waits for them, and re-layouts  4.82 us (4%)
  other arithmetic  1.79 us (2%)
    pallas_call x1, Pallas kernels, on_device(): pl.pallas_call(kernel, out_shape=jax.ShapeDtypeStruct((steps, rows, cols)...  107 us
    unnamed x3, local copies, waits for them, and re-layouts  2.84 us

profile of v4, /device:TPU:0, one launch (start us, length us, event | category | flops | bytes accessed | tf_op | source)
XLA Modules:
  0.0 114.5 jit_solution(17171833343519072367)
XLA Ops:
  0.6 0.7 copy.10
  1.4 0.1 reshape.28
  1.4 0.6 copy.11
  2.0 1.5 %copy.9 = f32[4,4,16,2]{3,2,1,0:T(8,128)} copy(f32[4,4,16,2]{2,3,1,0:T(2,128)} %param.7) | data formatting | bytes 4096 | tf_op args[1]
  3.6 107.3 %filter_grads.1 = bf16[6,128,1024]{2,1,0:T(8,128)(2,1)} custom-call(bf16[256,1024]{1,0:T(8,128)(2,1)} %bitcast.22, f32[256,2]{1,0:T(8,128)} %bitcast.21, s32[1,512]{1,0:T(1,128)} %bitcast.23, bf16[512,1024]{1,0:T(8,128)(2,1)} %bitcast.19, bf16[512,1024]{1,0:T(8,128)(2,1)} %bitcast.20, bf16[3,1024,1024]{2,1,0:T(8,128)(2,1)} %refs_0_.1), custom_call_target="tpu_custom_call" | custom-call | tf_op jit(solution)/shard_map/filter_grads/pallas_call | solution.py:477
  110.9 1.8 %convert_bitcast_fusion = f32[2,128,3,1024]{3,1,2,0:T(8,128)S(1)} fusion(bf16[2,3,128,1024]{3,2,1,0:T(8,128)(2,1)} %bitcast.18), kind=kLoop, calls=%fused_computation | loop fusion | flops 786432 | bytes 4718592 | tf_op jit(solution)/shard_map/transpose | solution.py:527
  112.7 1.9 %slice_bitcast_fusion = (f32[128,3,1024]{2,0,1:T(8,128)}, f32[128,3,1024]{2,0,1:T(8,128)}) fusion(f32[2,128,3,1024]{3,1,2,0:T(8,128)S(1)} %convert_bitcast_fusion), kind=kLoop, calls=%fused_computation.1 | loop fusion | bytes 6291456 | tf_op jit(solution)/shard_map/squeeze | solution.py:528
